TPU v7x, 256 devices: a whole 4x4x8 slice. The times are simulated.
256 devices in a mesh: src: 64 (over z, y, core), rhs: 4 (over x).
Axes of the slice: x: 4, y: 4, z: 8, core: 2. Of those that a mesh axis runs over, the one named last changes fastest.
Arguments:
- coefficients: bfloat16 [4096, 256, 64], P('src', 'rhs'), may hold values from -6 to 6
- pairing: int32 [8, 64, 64], P(None, 'src'), may hold values from 0 to 63, each once within a row
- level_weights: bfloat16 [8, 4096, 64, 128], P(None, 'src'), may hold values from -0.5 to 0.5
- middle_weights: bfloat16 [4096, 64, 64], P('src'), may hold values from -0.75 to 0.75
Outputs:
- target_coefficients: bfloat16 [4096, 256, 64], P('src', 'rhs')
Inputs may be any that keep to these rules, and one draw needn't show every extreme that they name: Each row pairing[l, d, :] is a permutation of 0 to 63.
All inputs are finite; a program needn't handle non-finite values.
Results may differ from a plain program's by a relative error of at most 0.014.
Values may be sent and summed in bfloat16 or wider, within the bound.
A program may use at most 64 MiB of HBM per device.

v0:
```python
import jax
import jax.numpy as jnp
from jax import lax
from jax.sharding import PartitionSpec as P

LEVELS = 8


def swapped(value, axis, apart):
    return lax.ppermute(value, axis, [(i, i ^ 1 << apart) for i in range(lax.axis_size(axis))])


def combine_blocks(state, other, weight, width):
    own = jnp.einsum(
        "bcj,bkj->bck", state, weight[:, :, :width], preferred_element_type=jnp.float32
    )
    far = jnp.einsum(
        "bcj,bkj->bck", other, weight[:, :, width:], preferred_element_type=jnp.float32
    )
    return (own + far).astype(jnp.bfloat16)


def level_step(state, pairing, level_weights, level, bits):
    weight = level_weights[level]
    width = state.shape[2]
    order = pairing[level, 0]
    other = swapped(state, "src", level % bits)
    other = jnp.take(other, order, axis=0)
    return combine_blocks(state, other, weight, width)


def body(coefficients, pairing, level_weights, middle_weights):
    bits = lax.axis_size("src").bit_length() - 1
    half = LEVELS // 2
    state = coefficients
    for level in range(half):
        state = level_step(state, pairing, level_weights, level, bits)
    moved = lax.all_to_all(state, "src", split_axis=0, concat_axis=0, tiled=True)
    state = jnp.einsum(
        "bcj,bkj->bck", moved, middle_weights, preferred_element_type=jnp.float32
    ).astype(jnp.bfloat16)
    for level in range(half, LEVELS):
        state = level_step(state, pairing, level_weights, level, bits)
    return state


def solution(mesh):
    placed = (
        P("src", "rhs", None),
        P(None, "src", None),
        P(None, "src", None, None),
        P("src", None, None),
    )
    return jax.shard_map(
        body, mesh=mesh, in_specs=placed, out_specs=P("src", "rhs", None), check_vma=False
    )
```

profile of v0, /device:TPU:17, one launch (start us, length us, event | category | flops | bytes accessed | tf_op | source)
XLA Modules:
  0.0 294.3 jit_solution(11493056527587471192)
XLA Ops:
  0.0 0.0 copy-start
  0.0 0.0 copy-start.7
  0.0 0.0 copy-start.8
  0.0 0.8 collective-permute-start
  0.8 6.2 %slice_bitcast_fusion = (bf16[64,64,128]{2,1,0:T(8,128)(2,1)S(1)}, bf16[64,64,128]{2,1,0:T(8,128)(2,1)}, bf16[64,64,128]{2,1,0:T(8,128)(2,1)}, bf16[64,64,128]{2...) fusion(bf16[8,64,64,128]{3,2,1,0:T(8,128)(2,1)} %param.8), kind=kLoop, calls=%fused_computation.49 | loop fusion | bytes 16777216 | tf_op jit(solution)/shard_map/squeeze | solution.py:24
  6.9 0.0 copy-done.8
  7.0 0.0 copy-start.6
  7.0 0.0 copy-done.7
  7.0 2.0 fusion.22
  9.0 0.0 copy-done.6
  9.0 0.0 collective-permute-done
  9.0 3.0 %gather_fusion = bf16[64,64,64]{2,1,0:T(8,128)(2,1)} fusion(bf16[64,64,64]{2,1,0:T(8,128)(2,1)} %collective-permute-done, s32[1024]{0:T(1024)S(1)} %pad_clamp_fusion.7), kind=kCustom, calls=%fused_computation.clone | custom fusion | bytes 1048832 | tf_op jit(solution)/shard_map/jit(_take)/gather | solution.py:28
  12.0 0.0 copy-start.5
  12.0 3.1 %add_convert_fusion.7 = bf16[64,64,64]{2,1,0:T(8,128)(2,1)S(1)} fusion(f32[64,64,64]{2,1,0:T(8,128)} %fusion.22, bf16[64,64,128]{2,1,0:T(8,128)(2,1)} %copy-done.6, bf16[64,64,64]{2,1,0:T(8,128)(2,1)} %gather_fusion, pred[64]{0:T(512)(128)(4,1)S(1)} %get-tuple-element.40), kind=kOutput, calls=%fused_computation.15 | convolution fusion | flops 34340864 | bytes 3145792 | tf_op jit(solution)/shard_map/bcj,bkj->bck/dot_general | solution.py:17
  15.1 1.1 collective-permute-start.1
  16.2 0.0 copy-done.5
  16.2 2.0 fusion.19
  18.2 21.7 %collective-permute-done.1 = bf16[64,64,64]{2,1,0:T(8,128)(2,1)} collective-permute-done((bf16[64,64,64]{2,1,0:T(8,128)(2,1)S(1)}, bf16[64,64,64]{2,1,0:T(8,128)(2,1)}, u32[]{:S(2)}, u32[]{:S(2)}) %collective-permute-start.1) | collective-permute-done | bytes 524320 | tf_op jit(solution)/shard_map/ppermute | solution.py:10
  39.9 2.9 gather_fusion.1
  42.8 0.0 copy-start.4
  42.8 3.1 %add_convert_fusion.6 = bf16[64,64,64]{2,1,0:T(8,128)(2,1)S(1)} fusion(f32[64,64,64]{2,1,0:T(8,128)} %fusion.19, bf16[64,64,128]{2,1,0:T(8,128)(2,1)} %get-tuple-element.27, bf16[64,64,64]{2,1,0:T(8,128)(2,1)} %gather_fusion.1, pred[64]{0:T(512)(128)(4,1)S(1)} %get-tuple-element.38), kind=kOutput, calls=%fused_computation.14 | convolution fusion | flops 34340864 | bytes 3145792 | tf_op jit(solution)/shard_map/bcj,bkj->bck/dot_general | solution.py:17
  45.8 1.8 collective-permute-start.2
  47.6 0.0 copy-done.4
  47.6 2.0 fusion.16
  49.6 21.6 %collective-permute-done.2 = bf16[64,64,64]{2,1,0:T(8,128)(2,1)} collective-permute-done((bf16[64,64,64]{2,1,0:T(8,128)(2,1)S(1)}, bf16[64,64,64]{2,1,0:T(8,128)(2,1)}, u32[]{:S(2)}, u32[]{:S(2)}) %collective-permute-start.2) | collective-permute-done | bytes 524320 | tf_op jit(solution)/shard_map/ppermute | solution.py:10
  71.3 2.9 gather_fusion.2
  74.2 0.0 copy-start.3
  74.2 3.1 %add_convert_fusion.5 = bf16[64,64,64]{2,1,0:T(8,128)(2,1)S(1)} fusion(f32[64,64,64]{2,1,0:T(8,128)} %fusion.16, bf16[64,64,128]{2,1,0:T(8,128)(2,1)} %get-tuple-element.26, bf16[64,64,64]{2,1,0:T(8,128)(2,1)} %gather_fusion.2, pred[64]{0:T(512)(128)(4,1)S(1)} %get-tuple-element.36), kind=kOutput, calls=%fused_computation.13 | convolution fusion | flops 34340864 | bytes 3145792 | tf_op jit(solution)/shard_map/bcj,bkj->bck/dot_general | solution.py:17
  77.3 1.7 collective-permute-start.3
  79.0 0.0 copy-done.3
  79.0 2.0 fusion.13
  81.0 19.6 %collective-permute-done.3 = bf16[64,64,64]{2,1,0:T(8,128)(2,1)} collective-permute-done((bf16[64,64,64]{2,1,0:T(8,128)(2,1)S(1)}, bf16[64,64,64]{2,1,0:T(8,128)(2,1)}, u32[]{:S(2)}, u32[]{:S(2)}) %collective-permute-start.3) | collective-permute-done | bytes 524320 | tf_op jit(solution)/shard_map/ppermute | solution.py:10
  100.6 2.9 gather_fusion.3
  103.5 4.0 %add_convert_fusion.4 = bf16[64,64,64]{2,1,0:T(8,128)(2,1)} fusion(f32[64,64,64]{2,1,0:T(8,128)} %fusion.13, bf16[64,64,128]{2,1,0:T(8,128)(2,1)} %get-tuple-element.25, bf16[64,64,64]{2,1,0:T(8,128)(2,1)} %gather_fusion.3, pred[64]{0:T(512)(128)(4,1)S(1)} %get-tuple-element.34), kind=kOutput, calls=%fused_computation.12 | convolution fusion | flops 34340864 | bytes 3145792 | tf_op jit(solution)/shard_map/bcj,bkj->bck/dot_general | solution.py:17
  107.5 3.0 %reshape.93 = bf16[64,2,2048]{2,1,0:T(2,128)(2,1)} reshape(bf16[64,64,64]{2,1,0:T(8,128)(2,1)} %add_convert_fusion.4) | data formatting | bytes 1048576
  110.5 30.9 %all_to_all.5 = bf16[64,2,2048]{2,1,0:T(2,128)(2,1)} all-to-all(bf16[64,2,2048]{2,1,0:T(2,128)(2,1)} %reshape.93), channel_id=1, replica_groups=mesh['src'=64,'rhs'=4] {'src'}, dimensions={0} | all-to-all | bytes 1048576 | tf_op jit(solution)/shard_map/all_to_all | solution.py:38
  141.4 3.0 %reshape.94 = bf16[64,64,64]{2,1,0:T(8,128)(2,1)} reshape(bf16[64,2,2048]{2,1,0:T(2,128)(2,1)} %all_to_all.5) | data formatting | bytes 1048576
  144.5 0.0 copy-done
  144.5 0.0 copy-start.2
  144.5 2.0 convolution_convert_fusion
  146.4 0.4 collective-permute-start.4
  146.9 0.0 copy-done.2
  146.9 2.0 fusion.10
  148.9 45.2 %collective-permute-done.4 = bf16[64,64,64]{2,1,0:T(8,128)(2,1)} collective-permute-done((bf16[64,64,64]{2,1,0:T(8,128)(2,1)S(1)}, bf16[64,64,64]{2,1,0:T(8,128)(2,1)}, u32[]{:S(2)}, u32[]{:S(2)}) %collective-permute-start.4) | collective-permute-done | bytes 524320 | tf_op jit(solution)/shard_map/ppermute | solution.py:10
  194.1 2.9 gather_fusion.4
  197.0 0.0 copy-start.1
  197.0 3.1 %add_convert_fusion.3 = bf16[64,64,64]{2,1,0:T(8,128)(2,1)S(1)} fusion(f32[64,64,64]{2,1,0:T(8,128)} %fusion.10, bf16[64,64,128]{2,1,0:T(8,128)(2,1)} %get-tuple-element.24, bf16[64,64,64]{2,1,0:T(8,128)(2,1)} %gather_fusion.4, pred[64]{0:T(512)(128)(4,1)S(1)} %get-tuple-element.32), kind=kOutput, calls=%fused_computation.11 | convolution fusion | flops 34340864 | bytes 3145792 | tf_op jit(solution)/shard_map/bcj,bkj->bck/dot_general | solution.py:17
  200.1 1.3 collective-permute-start.5
  201.4 0.0 copy-done.1
  201.4 2.0 fusion.7
  203.4 45.6 %collective-permute-done.5 = bf16[64,64,64]{2,1,0:T(8,128)(2,1)} collective-permute-done((bf16[64,64,64]{2,1,0:T(8,128)(2,1)S(1)}, bf16[64,64,64]{2,1,0:T(8,128)(2,1)}, u32[]{:S(2)}, u32[]{:S(2)}) %collective-permute-start.5) | collective-permute-done | bytes 524320 | tf_op jit(solution)/shard_map/ppermute | solution.py:10
  249.0 2.9 gather_fusion.5
  251.9 3.0 %add_convert_fusion.2 = bf16[64,64,64]{2,1,0:T(8,128)(2,1)S(1)} fusion(f32[64,64,64]{2,1,0:T(8,128)} %fusion.7, bf16[64,64,128]{2,1,0:T(8,128)(2,1)} %get-tuple-element.23, bf16[64,64,64]{2,1,0:T(8,128)(2,1)} %gather_fusion.5, pred[64]{0:T(512)(128)(4,1)S(1)} %get-tuple-element.30), kind=kOutput, calls=%fused_computation.10 | convolution fusion | flops 34340864 | bytes 3145792 | tf_op jit(solution)/shard_map/bcj,bkj->bck/dot_general | solution.py:17
  254.9 1.5 collective-permute-start.6
  256.4 2.0 fusion.4
  258.4 0.4 collective-permute-done.6
  258.8 2.9 gather_fusion.6
  261.7 2.7 add_convert_fusion.1
  264.4 0.8 collective-permute-start.7
  265.2 2.0 fusion.1
  267.2 21.8 %collective-permute-done.7 = bf16[64,64,64]{2,1,0:T(8,128)(2,1)} collective-permute-done((bf16[64,64,64]{2,1,0:T(8,128)(2,1)S(1)}, bf16[64,64,64]{2,1,0:T(8,128)(2,1)}, u32[]{:S(2)}, u32[]{:S(2)}) %collective-permute-start.7) | collective-permute-done | bytes 524320 | tf_op jit(solution)/shard_map/ppermute | solution.py:10
  289.0 2.0 gather_fusion.7
  291.0 3.3 %add_convert_fusion = bf16[64,64,64]{2,1,0:T(8,128)(2,1)} fusion(f32[64,64,64]{2,1,0:T(8,128)} %fusion.1, bf16[64,64,128]{2,1,0:T(8,128)(2,1)S(1)} %get-tuple-element.22, bf16[64,64,64]{2,1,0:T(8,128)(2,1)S(1)} %gather_fusion.7, pred[64]{0:T(512)(128)(4,1)S(1)} %get-tuple-element.6), kind=kOutput, calls=%fused_computation.8 | convolution fusion | flops 34340864 | bytes 3145792 | tf_op jit(solution)/shard_map/bcj,bkj->bck/dot_general | solution.py:17
  (9 shorter events, 0.1 us)
Async XLA Ops:
  0.0 144.5 %copy-start = (bf16[64,64,64]{2,1,0:T(8,128)(2,1)S(1)}, bf16[64,64,64]{2,1,0:T(8,128)(2,1)}, u32[]{:S(2)}) copy-start(bf16[64,64,64]{2,1,0:T(8,128)(2,1)} %param.9) | copy-start | bytes 1572868
  0.0 7.0 %copy-start.7 = (bf16[64,64,64]{2,1,0:T(8,128)(2,1)S(1)}, bf16[64,64,64]{2,1,0:T(8,128)(2,1)}, u32[]{:S(2)}) copy-start(bf16[64,64,64]{2,1,0:T(8,128)(2,1)} %param.6) | copy-start | bytes 1572868
  0.0 6.9 %copy-start.8 = (s32[8,1,64]{2,1,0:T(1,128)S(1)}, s32[8,1,64]{2,1,0:T(1,128)}, u32[]{:S(2)}) copy-start(s32[8,1,64]{2,1,0:T(1,128)} %param.7) | copy-start | bytes 6148
  0.0 9.0 %collective-permute-start = (bf16[64,64,64]{2,1,0:T(8,128)(2,1)}, bf16[64,64,64]{2,1,0:T(8,128)(2,1)}, u32[]{:S(2)}, u32[]{:S(2)}) collective-permute-start(bf16[64,64,64]{2,1,0:T(8,128)(2,1)} %param.6), channel_id=1, source_target_pairs={{0,4},{4,0},{8,12},{12,8},{16,20},{20,16},{24,28},{28,24},{32,36},... | collective-permute-start | bytes 1572872 | tf_op jit(solution)/shard_map/ppermute | solution.py:10
  7.0 2.1 copy-start.6
  12.0 4.2 %copy-start.5 = (bf16[64,64,128]{2,1,0:T(8,128)(2,1)S(1)}, bf16[64,64,128]{2,1,0:T(8,128)(2,1)}, u32[]{:S(2)}) copy-start(bf16[64,64,128]{2,1,0:T(8,128)(2,1)} %get-tuple-element.27) | copy-start | bytes 3145732
  15.1 24.8 %collective-permute-start.1 = (bf16[64,64,64]{2,1,0:T(8,128)(2,1)S(1)}, bf16[64,64,64]{2,1,0:T(8,128)(2,1)}, u32[]{:S(2)}, u32[]{:S(2)}) collective-permute-start(bf16[64,64,64]{2,1,0:T(8,128)(2,1)S(1)} %add_convert_fusion.7), channel_id=1, source_target_pairs={{0,8},{4,12},{8,0},{12,4},{16,24},{20,28},{24,16},{28,20},{32,40},... | collective-permute-start | bytes 1572872 | tf_op jit(solution)/shard_map/ppermute | solution.py:10
  42.8 4.9 %copy-start.4 = (bf16[64,64,128]{2,1,0:T(8,128)(2,1)S(1)}, bf16[64,64,128]{2,1,0:T(8,128)(2,1)}, u32[]{:S(2)}) copy-start(bf16[64,64,128]{2,1,0:T(8,128)(2,1)} %get-tuple-element.26) | copy-start | bytes 3145732
  45.8 25.4 %collective-permute-start.2 = (bf16[64,64,64]{2,1,0:T(8,128)(2,1)S(1)}, bf16[64,64,64]{2,1,0:T(8,128)(2,1)}, u32[]{:S(2)}, u32[]{:S(2)}) collective-permute-start(bf16[64,64,64]{2,1,0:T(8,128)(2,1)S(1)} %add_convert_fusion.6), channel_id=1, source_target_pairs={{0,16},{4,20},{8,24},{12,28},{16,0},{20,4},{24,8},{28,12},{32,48},... | collective-permute-start | bytes 1572872 | tf_op jit(solution)/shard_map/ppermute | solution.py:10
  74.2 4.8 %copy-start.3 = (bf16[64,64,128]{2,1,0:T(8,128)(2,1)S(1)}, bf16[64,64,128]{2,1,0:T(8,128)(2,1)}, u32[]{:S(2)}) copy-start(bf16[64,64,128]{2,1,0:T(8,128)(2,1)} %get-tuple-element.25) | copy-start | bytes 3145732
  77.3 23.3 %collective-permute-start.3 = (bf16[64,64,64]{2,1,0:T(8,128)(2,1)S(1)}, bf16[64,64,64]{2,1,0:T(8,128)(2,1)}, u32[]{:S(2)}, u32[]{:S(2)}) collective-permute-start(bf16[64,64,64]{2,1,0:T(8,128)(2,1)S(1)} %add_convert_fusion.5), channel_id=1, source_target_pairs={{0,32},{4,36},{8,40},{12,44},{16,48},{20,52},{24,56},{28,60},{32,0... | collective-permute-start | bytes 1572872 | tf_op jit(solution)/shard_map/ppermute | solution.py:10
  144.5 2.4 copy-start.2
  146.4 47.7 %collective-permute-start.4 = (bf16[64,64,64]{2,1,0:T(8,128)(2,1)S(1)}, bf16[64,64,64]{2,1,0:T(8,128)(2,1)}, u32[]{:S(2)}, u32[]{:S(2)}) collective-permute-start(bf16[64,64,64]{2,1,0:T(8,128)(2,1)S(1)} %convolution_convert_fusion), channel_id=1, source_target_pairs={{0,64},{4,68},{8,72},{12,76},{16,80},{20,84},{24,88},{28,92},{32,9... | collective-permute-start | bytes 1572872 | tf_op jit(solution)/shard_map/ppermute | solution.py:10
  197.0 4.4 %copy-start.1 = (bf16[64,64,128]{2,1,0:T(8,128)(2,1)S(1)}, bf16[64,64,128]{2,1,0:T(8,128)(2,1)}, u32[]{:S(2)}) copy-start(bf16[64,64,128]{2,1,0:T(8,128)(2,1)} %get-tuple-element.23) | copy-start | bytes 3145732
  200.1 48.9 %collective-permute-start.5 = (bf16[64,64,64]{2,1,0:T(8,128)(2,1)S(1)}, bf16[64,64,64]{2,1,0:T(8,128)(2,1)}, u32[]{:S(2)}, u32[]{:S(2)}) collective-permute-start(bf16[64,64,64]{2,1,0:T(8,128)(2,1)S(1)} %add_convert_fusion.3), channel_id=1, source_target_pairs={{0,128},{4,132},{8,136},{12,140},{16,144},{20,148},{24,152},{28,15... | collective-permute-start | bytes 1572872 | tf_op jit(solution)/shard_map/ppermute | solution.py:10
  254.9 3.9 %collective-permute-start.6 = (bf16[64,64,64]{2,1,0:T(8,128)(2,1)S(1)}, bf16[64,64,64]{2,1,0:T(8,128)(2,1)}, u32[]{:S(2)}, u32[]{:S(2)}) collective-permute-start(bf16[64,64,64]{2,1,0:T(8,128)(2,1)S(1)} %add_convert_fusion.2), channel_id=1, source_target_pairs={{0,4},{4,0},{8,12},{12,8},{16,20},{20,16},{24,28},{28,24},{32,36},... | collective-permute-start | bytes 1572872 | tf_op jit(solution)/shard_map/ppermute | solution.py:10
  264.4 24.6 %collective-permute-start.7 = (bf16[64,64,64]{2,1,0:T(8,128)(2,1)S(1)}, bf16[64,64,64]{2,1,0:T(8,128)(2,1)}, u32[]{:S(2)}, u32[]{:S(2)}) collective-permute-start(bf16[64,64,64]{2,1,0:T(8,128)(2,1)S(1)} %add_convert_fusion.1), channel_id=1, source_target_pairs={{0,8},{4,12},{8,0},{12,4},{16,24},{20,28},{24,16},{28,20},{32,40},... | collective-permute-start | bytes 1572872 | tf_op jit(solution)/shard_map/ppermute | solution.py:10
where the time goes:
time: 297 us; the launch traced here: 294 us
  waiting for transfers between devices  176 us (59%)
  matrix products  43.3 us (15%)
  local copies, waits for them, and re-layouts  34.5 us (12%)
  blocking collectives  30.9 us (10%)
  starting transfers between devices  9.38 us (3%)
    ppermute x8, waiting for transfers between devices, swapped(): lax.ppermute(value, axis, [(i, i ^ 1 << apart) for i in range(lax.axis_si...  176 us
    all_to_all x1, blocking collectives, body(): lax.all_to_all(state, 'src', split_axis=0, concat_axis=0, tiled=True)  30.9 us
    dot_general x8, matrix products, combine_blocks(): jnp.einsum('bcj,bkj->bck', other, weight[:, :, width:], preferred_element...  25.3 us
    gather x8, local copies, waits for them, and re-layouts, level_step(): other = jnp.take(other, order, axis=0)  22.3 us
    dot_general x8, matrix products, combine_blocks(): jnp.einsum('bcj,bkj->bck', state, weight[:, :, :width], preferred_element...  16.1 us
    ppermute x8, starting transfers between devices, swapped(): lax.ppermute(value, axis, [(i, i ^ 1 << apart) for i in range(lax.axis_si...  9.38 us
    squeeze x1, local copies, waits for them, and re-layouts, level_step(): weight = level_weights[level]  6.17 us
    unnamed x20, local copies, waits for them, and re-layouts  6.07 us
  transfers between devices with their start and end apart: 8, of which 7 were waited for; matrix products, arithmetic and copies ran while one was open for 8% of the time, Pallas kernels for 0%

commit v1 on v0

v1 whole, which is shorter than its diff:
```python
import functools

import jax
import jax.numpy as jnp
from jax import lax
from jax.experimental import pallas as pl
from jax.experimental.pallas import tpu as pltpu
from jax.sharding import PartitionSpec as P

LEVELS = 8
HALF = 4
BITS = 6
B = 64
K = 64
C = 64
Q = 2
R = C // Q // 2
PIECES = 4
PB = B // PIECES
MESH = pl.DeviceIdType.MESH


def kernel(coef, pairing, lw, mw, out, x_in, w, m, st, t1, mv, y_out,
           in_sem, w_sem, m_sem, out_sem, lvl_send, lvl_recv, z_send, z_recv, y_send, y_recv, own_sem, *rv):
    me = lax.axis_index("src")
    rhs = lax.axis_index("rhs")
    z, yc = me // 8, me % 8

    load_x = pltpu.make_async_copy(coef, x_in, in_sem)
    load_x.start()
    load_w = [pltpu.make_async_copy(lw.at[l], w.at[l], w_sem.at[l]) for l in range(LEVELS)]
    load_m = pltpu.make_async_copy(mw, m, m_sem)

    def at(s):
        return (s, rhs)

    def partner(h):
        return me + (1 << h) * (1 - 2 * ((me // (1 << h)) % 2))

    z_peers = [((z + k) % 8) * 8 + yc for k in range(1, 8)]
    y_peers = [z * 8 + (yc + k) % 8 for k in range(1, 8)]
    barrier = pltpu.get_barrier_semaphore()
    for s in z_peers + y_peers:
        pl.semaphore_signal(barrier, inc=1, device_id=at(s), device_id_type=MESH)
    for l in range(HALF):
        load_w[l].start()
    load_m.start()
    for l in range(HALF, LEVELS):
        load_w[l].start()

    def level_copy(l, q, piece):
        blocks = pl.ds(piece * PB, PB)
        src = st.at[l if l < HALF else l + 1, q, blocks]
        return pltpu.make_async_remote_copy(
            src_ref=src, dst_ref=rv[l * Q + q].at[blocks],
            send_sem=lvl_send.at[l, q, piece], recv_sem=lvl_recv.at[l, q, piece],
            device_id=at(partner(l % BITS)), device_id_type=MESH)

    def z_copy(q, k):
        return pltpu.make_async_remote_copy(
            src_ref=st.at[HALF, q, pl.ds(((z + k) % 8) * 8, 8)], dst_ref=t1.at[q, z],
            send_sem=z_send.at[q, k], recv_sem=z_recv.at[q, k],
            device_id=at(z_peers[k - 1]), device_id_type=MESH)

    def y_copy(q, k):
        return pltpu.make_async_remote_copy(
            src_ref=t1.at[q, :, (yc + k) % 8], dst_ref=mv.at[q, :, yc],
            send_sem=y_send.at[q, k], recv_sem=y_recv.at[q, k],
            device_id=at(y_peers[k - 1]), device_id_type=MESH)

    lane = lax.broadcasted_iota(jnp.int32, (K, 2 * K), 1)
    low = lane < K

    def spread(pair):
        zero = jnp.zeros_like(pair)
        turned = jnp.concatenate([pair[:, K:], pair[:, :K]], axis=1)
        top = jnp.concatenate([jnp.where(low, pair, zero), jnp.where(low, turned, zero)], axis=1)
        bottom = jnp.concatenate([jnp.where(low, zero, turned), jnp.where(low, zero, pair)], axis=1)
        return jnp.concatenate([top, bottom], axis=0)

    def times(x, weight):
        return lax.dot_general(x, weight, (((1,), (1,)), ((), ())), preferred_element_type=jnp.float32)

    def level(l, q):
        src = l if l < HALF else l + 1
        @pl.loop(0, PIECES)
        def _(piece):
            level_copy(l, q, piece).wait_recv()

        @pl.loop(0, PIECES)
        def _(piece):
            for i in range(PB):
                b = piece * PB + i
                own = st[src, q, b]
                far = rv[l * Q + q][pairing[l, 0, b]]
                acc = times(jnp.concatenate([own, far], axis=1), spread(w[l, b]))
                new = acc.astype(jnp.bfloat16)
                if l < LEVELS - 1:
                    st[src + 1, q, b] = new
                else:
                    y_out[b, pl.ds(q * 2 * R, R), :] = new[:, :K]
                    y_out[b, pl.ds(q * 2 * R + R, R), :] = new[:, K:]
            if l < LEVELS - 1 and l != HALF - 1:
                level_copy(l + 1, q, piece).start()

    load_x.wait()
    for q in range(Q):
        @pl.loop(0, PIECES)
        def _(piece):
            for i in range(PB):
                b = piece * PB + i
                st[0, q, b] = jnp.concatenate(
                    [x_in[b, q * 2 * R:q * 2 * R + R, :], x_in[b, q * 2 * R + R:(q + 1) * 2 * R, :]], axis=1)

    pl.semaphore_wait(barrier, 14)
    for q in range(Q):
        @pl.loop(0, PIECES)
        def _(piece):
            level_copy(0, q, piece).start()

    for l in range(HALF):
        load_w[l].wait()
        for q in range(Q):
            level(l, q)
            if l == HALF - 1:
                for k in (4, 3, 5, 2, 6, 1, 7):
                    z_copy(q, k).start()
                own = pltpu.make_async_copy(st.at[HALF, q, pl.ds(z * 8, 8)], t1.at[q, z], own_sem.at[0, q])
                own.start()

    load_m.wait()
    for q in range(Q):
        for k in range(1, 8):
            z_copy(q, k).wait_recv()
        pltpu.make_async_copy(st.at[HALF, q, pl.ds(z * 8, 8)], t1.at[q, z], own_sem.at[0, q]).wait()
        for k in (4, 3, 5, 2, 6, 1, 7):
            y_copy(q, k).start()
        pltpu.make_async_copy(t1.at[q, :, yc], mv.at[q, :, yc], own_sem.at[1, q]).start()

    for q in range(Q):
        for k in range(1, 8):
            y_copy(q, k).wait_recv()
        pltpu.make_async_copy(t1.at[q, :, yc], mv.at[q, :, yc], own_sem.at[1, q]).wait()

        @pl.loop(0, PIECES)
        def _(piece):
            for i in range(PB):
                b = piece * PB + i
                mb = m[b]
                zero = jnp.zeros_like(mb)
                weight = jnp.concatenate(
                    [jnp.concatenate([mb, zero], axis=1), jnp.concatenate([zero, mb], axis=1)], axis=0)
                st[HALF + 1, q, b] = times(mv[q, piece * (PB // 8) + i // 8, i % 8], weight).astype(jnp.bfloat16)
            level_copy(HALF, q, piece).start()

    for l in range(HALF, LEVELS):
        load_w[l].wait()
        for q in range(Q):
            level(l, q)

    store = pltpu.make_async_copy(y_out, out, out_sem)
    store.start()
    for q in range(Q):
        for l in range(LEVELS):
            @pl.loop(0, PIECES)
            def _(piece):
                level_copy(l, q, piece).wait_send()
        for k in range(1, 8):
            z_copy(q, k).wait_send()
            y_copy(q, k).wait_send()
    store.wait()


def body(coefficients, pairing, level_weights, middle_weights):
    bf16 = jnp.bfloat16
    dma = pltpu.SemaphoreType.DMA
    any_space = pl.BlockSpec(memory_space=pl.ANY)
    return pl.pallas_call(
        kernel,
        out_shape=jax.ShapeDtypeStruct((B, C, K), bf16),
        in_specs=[any_space, pl.BlockSpec(memory_space=pltpu.SMEM), any_space, any_space],
        out_specs=any_space,
        scratch_shapes=[
            pltpu.VMEM((B, C, K), bf16),
            pltpu.VMEM((LEVELS, B, K, 2 * K), bf16),
            pltpu.VMEM((B, K, K), bf16),
            pltpu.VMEM((LEVELS + 1, Q, B, R, 2 * K), bf16),
            pltpu.VMEM((Q, 8, 8, R, 2 * K), bf16),
            pltpu.VMEM((Q, 8, 8, R, 2 * K), bf16),
            pltpu.VMEM((B, C, K), bf16),
            dma, dma((LEVELS,)), dma, dma,
            dma((LEVELS, Q, PIECES)), dma((LEVELS, Q, PIECES)),
            dma((Q, 8)), dma((Q, 8)), dma((Q, 8)), dma((Q, 8)), dma((2, Q)),
        ] + [pltpu.VMEM((B, R, 2 * K), bf16)] * (LEVELS * Q),
        compiler_params=pltpu.CompilerParams(
            collective_id=0, has_side_effects=True, vmem_limit_bytes=48 * 1024 * 1024),
    )(coefficients, pairing, level_weights, middle_weights)


def solution(mesh):
    placed = (
        P("src", "rhs", None),
        P(None, "src", None),
        P(None, "src", None, None),
        P("src", None, None),
    )
    return jax.shard_map(
        body, mesh=mesh, in_specs=placed, out_specs=P("src", "rhs", None), check_vma=False
    )
```

time: 297 us -> 129 us (0.43)
  waiting for transfers between devices: 176 us -> 0 us
  Pallas kernels: 0 us -> 123 us
  matrix products: 43.3 us -> 0 us
  blocking collectives: 30.9 us -> 0 us
  local copies, waits for them, and re-layouts: 34.5 us -> 4.11 us
  starting transfers between devices: 9.38 us -> 0 us
    ppermute x8 -> x0, waiting for transfers between devices: 176 us -> none  [swapped(): lax.ppermute(value, axis, [(i, i ^ 1 << apart) for i in range(lax.axis_si...]
    pallas_call x0 -> x1, Pallas kernels: none -> 123 us  [body(): pl.pallas_call(kernel, out_shape=jax.ShapeDtypeStruct((B, C, K), bf16), i...]
    dot_general x17 -> x0, matrix products: 43.3 us -> none  [the longest x8 25.3 us: combine_blocks(): jnp.einsum('bcj,bkj->bck', other, weight[:, :, width:], preferred_element...]
    all_to_all x1 -> x0, blocking collectives: 30.9 us -> none  [body(): lax.all_to_all(state, 'src', split_axis=0, concat_axis=0, tiled=True)]
    gather x8 -> x0, local copies, waits for them, and re-layouts: 22.3 us -> none  [level_step(): other = jnp.take(other, order, axis=0)]
    ppermute x8 -> x0, starting transfers between devices: 9.38 us -> none  [swapped(): lax.ppermute(value, axis, [(i, i ^ 1 << apart) for i in range(lax.axis_si...]
    squeeze x1 -> x0, local copies, waits for them, and re-layouts: 6.17 us -> none  [level_step(): weight = level_weights[level]]
    unnamed x20 -> x7, local copies, waits for them, and re-layouts: 6.07 us -> 4.11 us
  transfers between devices with their start and end apart: 8 -> 0, of which waited for: 7 -> 0; matrix products, arithmetic and copies ran while one was open for 8% -> 0% of each run, Pallas kernels for 0% -> 0%
where the time goes in v1:
time: 129 us; the launch traced here: 127 us
  Pallas kernels  123 us (95%)
  local copies, waits for them, and re-layouts  4.11 us (3%)
    pallas_call x1, Pallas kernels, body(): pl.pallas_call(kernel, out_shape=jax.ShapeDtypeStruct((B, C, K), bf16), i...  123 us
    unnamed x7, local copies, waits for them, and re-layouts  4.11 us

profile of v1, /device:TPU:17, one launch (start us, length us, event | category | flops | bytes accessed | tf_op | source)
XLA Modules:
  0.0 127.2 jit_solution(17572519968814771494)
XLA Ops:
  0.0 0.0 copy-start
  0.0 1.2 copy-done
  1.2 0.0 copy-start.1
  1.2 1.2 copy-done.1
  2.5 0.0 copy-start.2
  2.5 0.7 copy-done.2
  3.1 123.0 %shard_map.46 = bf16[64,64,64]{2,1,0:T(8,128)(2,1)S(1)} custom-call(bf16[64,64,64]{2,1,0:T(8,128)(2,1)S(1)} %copy-done, s32[8,1,64]{2,1,0:T(1,128)S(1)} %copy-done.2, bf16[8,64,64,128]{3,2,1,0:T(8,128)(2,1)} %lw.1, bf16[64,64,64]{2,1,0:T(8,128)(2,1)S(1)} %copy-done.1), custom_call_target="tpu_custom_call" | custom-call | tf_op jit(solution)/shard_map/pallas_call | solution.py:178
  126.2 1.0 copy.6
Async XLA Ops:
  0.0 1.2 copy-start
  1.2 1.2 copy-start.1
  2.5 0.7 copy-start.2

commit v2 on v0

v2 whole, which is shorter than its diff:
```python
import jax
import jax.numpy as jnp
from jax import lax
from jax.experimental import pallas as pl
from jax.experimental.pallas import tpu as pltpu
from jax.sharding import PartitionSpec as P

LEVELS = 8
N = 64
B = 64
K = 64
C = 64
Q = 2
H = C // Q // 2
PIECES = 4
PB = B // PIECES
PP = PB // 2
X = 4
MESH = pl.DeviceIdType.MESH
SKEW = 0


def kernel(coef, pairing, pairing_any, lw, mw, out,
           x_in, w, m, w_x, m_x, m_send, pair_v, pair_s, y_out,
           st0, st1, st2, st3, moved_from, st6, st7,
           in_sem, w_sem, m_sem, out_sem, pair_sem, own_sem,
           lvl_send, lvl_recv, a_send, a_recv, e_send, e_recv, wz_send, wz_recv, wx_send, wx_recv,
           *per_chunk):
    me = lax.axis_index("src")
    rhs = lax.axis_index("rhs")
    z = me // 8
    zb1 = (z // 2) % 2
    n_lists = 9
    r0, r1, r2, r3, r6, r7, mv, t4, far5 = [per_chunk[i * Q:(i + 1) * Q] for i in range(n_lists)]
    own5, oth5, ret5 = [per_chunk[(n_lists + i) * Q:(n_lists + i + 1) * Q] for i in range(3)]
    recv_of = {0: r0, 1: r1, 2: r2, 3: r3, 6: r6, 7: r7}
    state_of = {0: st0, 1: st1, 2: st2, 3: st3, 6: st6, 7: st7}

    load_x = pltpu.make_async_copy(coef, x_in, in_sem)
    load_x.start()
    load_w = [pltpu.make_async_copy(lw.at[l], w.at[l], w_sem.at[l]) for l in range(LEVELS)]
    load_m = pltpu.make_async_copy(mw, m, m_sem)
    load_m.start()

    def flipped(s, h):
        return s + (1 << h) * (1 - 2 * ((s // (1 << h)) % 2))

    far_x = [(rhs + k) % X for k in range(1, X)]
    barrier = pltpu.get_barrier_semaphore()

    @pl.loop(1, N)
    def _(k):
        pl.semaphore_signal(barrier, inc=1, device_id=((me + k) % N, rhs), device_id_type=MESH)

    for x in far_x:
        pl.semaphore_signal(barrier, inc=1, device_id=(me, x), device_id_type=MESH)
    for l in range(LEVELS):
        load_w[l].start()

    def remote(src, dst, send, recv, dev, x=None):
        return pltpu.make_async_remote_copy(
            src_ref=src, dst_ref=dst, send_sem=send, recv_sem=recv,
            device_id=(dev, rhs if x is None else x), device_id_type=MESH)

    def level_copy(l, q, piece):
        blocks = pl.ds(piece * PB, PB)
        return remote(state_of[l].at[q, blocks], recv_of[l][q].at[blocks],
                      lvl_send.at[l, q, piece], lvl_recv.at[l, q, piece], flipped(me, l % 6))

    def a2a_copy(q, e):
        return remote(moved_from.at[q, e], mv[q].at[me], a_send.at[q], a_recv.at[q], e)

    def a2a_all(q):
        return remote(moved_from.at[q, pl.ds(0, N - 1)], mv[q].at[pl.ds(0, N - 1)],
                      a_send.at[q], a_recv.at[q], flipped(me, 0))

    def a2a_own(q):
        return pltpu.make_async_copy(moved_from.at[q, me], mv[q].at[me], own_sem.at[q])

    def merged_copies(q, piece):
        pairs = pl.ds(piece * PP, PP)
        e16, e32 = flipped(me, 4), flipped(me, 5)
        e48 = flipped(e16, 5)
        return [
            remote(own5[q].at[pairs], far5[q].at[0, pairs], e_send.at[0, q, piece], e_recv.at[0, q, piece], e32),
            remote(oth5[q].at[pairs], far5[q].at[1, pairs], e_send.at[1, q, piece], e_recv.at[1, q, piece], e48),
            remote(oth5[q].at[pairs], ret5[q].at[pairs], e_send.at[2, q, piece], e_recv.at[2, q, piece], e16),
        ]

    quarter_w, quarter_m = pl.ds(rhs * (B // X), B // X), pl.ds(rhs * (B // 2 // X), B // 2 // X)

    def weight_z():
        e16 = flipped(me, 4)
        return [
            remote(m_send.at[quarter_m], m_x.at[quarter_m], wz_send.at[0], wz_recv.at[0], e16),
            remote(lw.at[4, quarter_w], w_x.at[quarter_w], wz_send.at[1], wz_recv.at[1], e16),
            remote(pairing_any, pair_v, wz_send.at[2], wz_recv.at[2], e16),
        ]

    def weight_x(which):
        ref, quarter = ((m_x, quarter_m), (w_x, quarter_w))[which]
        return [remote(ref.at[quarter], ref.at[quarter], wx_send.at[which, k], wx_recv.at[which, k], me, far_x[k])
                for k in range(X - 1)]

    low_w = lax.broadcasted_iota(jnp.int32, (K, 2 * K), 1) < K
    low_t = lax.broadcasted_iota(jnp.int32, (H, 2 * K), 1) < K

    def turned(x):
        return jnp.concatenate([x[:, K:], x[:, :K]], axis=1)

    def lo(x):
        return jnp.where(low_w, x, jnp.zeros_like(x))

    def hi(x):
        return jnp.where(low_w, jnp.zeros_like(x), x)

    def first_rows(pair):
        return jnp.concatenate([lo(pair), hi(pair)], axis=1)

    def second_rows(pair):
        back = turned(pair)
        return jnp.concatenate([hi(back), lo(back)], axis=1)

    def times(x, *rows):
        weight = jnp.concatenate(rows, axis=0)
        return lax.dot_general(x, weight, (((1,), (1,)), ((), ())), preferred_element_type=jnp.float32)

    def beside(own, far):
        return jnp.concatenate([own, far], axis=1)

    def plain(l, q, b, swap=False):
        own = state_of[l][q, b]
        far = turned(recv_of[l][q][pairing[l, 0, b]])
        rows = first_rows(w[l, b]), second_rows(w[l, b])
        return times(beside(own, far), *(rows[::-1] if swap else rows))

    def bf16(x):
        return x.astype(jnp.bfloat16)

    def begin(q):
        @pl.loop(0, PIECES)
        def _(piece):
            for i in range(PB):
                b = piece * PB + i
                st0[q, b] = beside(x_in[b, 2 * q * H:(2 * q + 1) * H, :], x_in[b, (2 * q + 1) * H:(2 * q + 2) * H, :])

    def send_level(l, q):
        @pl.loop(0, PIECES)
        def _(piece):
            level_copy(l, q, piece).start()

    def wait_level(l, q):
        @pl.loop(0, PIECES)
        def _(piece):
            level_copy(l, q, piece).wait_recv()

    def plain_level(l, q):
        wait_level(l, q)

        @pl.loop(0, PIECES)
        def _(piece):
            for i in range(PB):
                b = piece * PB + i
                new = bf16(plain(l, q, b))
                if l < LEVELS - 1:
                    state_of[l + 1][q, b] = new
                else:
                    at = pl.multiple_of(2 * q * H + zb1 * H, H)
                    y_out[b, pl.ds(at, H), :] = new[:, :K]
                    at = pl.multiple_of((2 * q + 1) * H - zb1 * H, H)
                    y_out[b, pl.ds(at, H), :] = new[:, K:]
            if l < LEVELS - 1:
                level_copy(l + 1, q, piece).start()

    def last_source_level(q):
        wait_level(3, q)

        @pl.loop(0, PIECES)
        def _(i):
            piece = (i + z // 2) % PIECES
            base = (piece // 2) * (N // 2) + (piece % 2) * PP
            for j in range(PP):
                b = base + j
                one = plain(3, q, b)
                two = plain(3, q, b + 16, swap=True)
                moved_from[q, b] = bf16(jnp.where(low_t, one, two))
                moved_from[q, b + 16] = bf16(jnp.where(low_t, two, one))

            @pl.loop(0, PP)
            def _(j):
                for e in (base + j, base + j + 16):
                    @pl.when(e != me)
                    def _():
                        a2a_copy(q, e).start()

                    @pl.when(e == me)
                    def _():
                        a2a_own(q).start()

    def middle_and_level4(q):
        a2a_all(q).wait_recv()
        a2a_own(q).wait()

        @pl.loop(0, PIECES)
        def _(piece):
            for j in range(PP):
                d = piece * PP + j
                theirs = m_x[d]
                zero = jnp.zeros((K, K), jnp.bfloat16)
                for s, other in ((d, hi(theirs)), (d + B // 2, hi(turned(theirs)))):
                    t4[q][s] = bf16(times(mv[q][s], beside(m[s], zero), other))

        @pl.loop(0, PIECES)
        def _(piece):
            for j in range(PP):
                i = piece * PP + j
                new = []
                for b, swap in ((i, False), (i + B // 2, True)):
                    far = jnp.where(low_t, t4[q][pair_s[4, 0, b]], t4[q][pairing[4, 0, b]])
                    rows = first_rows(w[4, b]), second_rows(w_x[b])
                    new.append(times(beside(t4[q][b], far), *(rows[::-1] if swap else rows)))
                own5[q][i] = bf16(jnp.where(low_t, new[0], new[1]))
                oth5[q][i] = bf16(jnp.where(low_t, new[1], new[0]))
            for copy in merged_copies(q, piece):
                copy.start()

    def level5(q):
        @pl.loop(0, PIECES)
        def _(piece):
            for copy in merged_copies(q, piece):
                copy.wait_recv()

        @pl.loop(0, PIECES)
        def _(piece):
            for j in range(PP):
                i = piece * PP + j
                for b, upper in ((i, 0), (i + B // 2, 1)):
                    mine, back = own5[q][i], ret5[q][i]
                    own = jnp.where(low_t, back, mine) if upper else jnp.where(low_t, mine, back)
                    p = pairing[5, 0, b]
                    at, half = p % (B // 2), p // (B // 2)
                    far = jnp.where(low_t, far5[q][half, at], far5[q][1 - half, at])
                    far = jnp.where(half == upper, turned(far), far)
                    rows = first_rows(w[5, b]), second_rows(w[5, b])
                    st6[q, b] = bf16(times(beside(own, far), *(rows[::-1] if upper else rows)))

        send_level(6, q)

    waited = set()

    def need(*names):
        for name in names:
            if name not in waited:
                waited.add(name)
                if name == "m":
                    load_m.wait()
                elif name == "x":
                    for which in range(2):
                        for copy in weight_x(which):
                            copy.wait_recv()
                    to_smem = pltpu.make_async_copy(pair_v, pair_s, pair_sem)
                    to_smem.start()
                    to_smem.wait()
                else:
                    load_w[name].wait()

    def forward():
        for which, crossing in enumerate(weight_z()):
            crossing.wait_recv()
            if which < 2:
                for copy in weight_x(which):
                    copy.start()

    def store(q):
        rows = pl.ds(2 * q * H, 2 * H)
        return pltpu.make_async_copy(y_out.at[:, rows], out.at[:, rows], out_sem.at[q])

    def task(t, q):
        if t < 3:
            need(t)
            plain_level(t, q)
        elif t == 3:
            need(3)
            last_source_level(q)
        elif t == 4:
            need("m", "x", 4)
            middle_and_level4(q)
        elif t == 5:
            need(5)
            level5(q)
        else:
            need(t)
            plain_level(t, q)
            if t == 7:
                store(q).start()
        if t == 1 and q == Q - 1:
            forward()

    load_x.wait()
    begin(0)
    pl.semaphore_wait(barrier, N - 1 + X - 1)
    send_level(0, 0)
    for q in range(1, Q):
        begin(q)
        send_level(0, q)
    need("m")
    for d in range(B // 2):
        m_send[d] = beside(m[d + B // 2], m[d])
    for copy in weight_z():
        copy.start()
    for _, q, t in sorted((t + SKEW * q, q, t) for q in range(Q) for t in range(8)):
        task(t, q)

    for copy in weight_z() + weight_x(0) + weight_x(1):
        copy.wait_send()
    for q in range(Q):
        @pl.loop(0, PIECES)
        def _(piece):
            for l in (0, 1, 2, 3, 6, 7):
                level_copy(l, q, piece).wait_send()
            for copy in merged_copies(q, piece):
                copy.wait_send()
        a2a_all(q).wait_send()
    for q in range(Q):
        store(q).wait()


def body(coefficients, pairing, level_weights, middle_weights):
    bf16 = jnp.bfloat16
    dma = pltpu.SemaphoreType.DMA
    any_space = pl.BlockSpec(memory_space=pl.ANY)
    tiles = pltpu.VMEM((Q, B, H, 2 * K), bf16)
    full = pltpu.VMEM((B, H, 2 * K), bf16)
    half = pltpu.VMEM((B // 2, H, 2 * K), bf16)
    both = pltpu.VMEM((2, B // 2, H, 2 * K), bf16)
    return pl.pallas_call(
        kernel,
        out_shape=jax.ShapeDtypeStruct((B, C, K), bf16),
        in_specs=[any_space, pl.BlockSpec(memory_space=pltpu.SMEM), any_space, any_space, any_space],
        out_specs=any_space,
        scratch_shapes=[
            pltpu.VMEM((B, C, K), bf16),
            pltpu.VMEM((LEVELS, B, K, 2 * K), bf16),
            pltpu.VMEM((B, K, K), bf16),
            pltpu.VMEM((B, K, 2 * K), bf16),
            pltpu.VMEM((B // 2, K, 2 * K), bf16),
            pltpu.VMEM((B // 2, K, 2 * K), bf16),
            pltpu.VMEM((LEVELS, 1, B), jnp.int32),
            pltpu.SMEM((LEVELS, 1, B), jnp.int32),
            pltpu.VMEM((B, C, K), bf16),
        ] + [tiles] * 7 + [
            dma, dma((LEVELS,)), dma, dma((Q,)), dma, dma((Q,)),
            dma((LEVELS, Q, PIECES)), dma((LEVELS, Q, PIECES)), dma((Q,)), dma((Q,)),
            dma((3, Q, PIECES)), dma((3, Q, PIECES)), dma((3,)), dma((3,)), dma((2, X - 1)), dma((2, X - 1)),
        ] + [full] * (8 * Q) + [both] * Q + [half] * (3 * Q),
        compiler_params=pltpu.CompilerParams(
            collective_id=0, has_side_effects=True, vmem_limit_bytes=60 * 1024 * 1024),
    )(coefficients, pairing, pairing, level_weights, middle_weights)


def solution(mesh):
    placed = (
        P("src", "rhs", None),
        P(None, "src", None),
        P(None, "src", None, None),
        P("src", None, None),
    )
    return jax.shard_map(
        body, mesh=mesh, in_specs=placed, out_specs=P("src", "rhs", None), check_vma=False
    )
```

time: 297 us -> 105 us (0.35)
  the two profiles are of different devices: /device:TPU:17 before, /device:TPU:8 now
where the time goes in v2:
time: 105 us; the launch traced here: 104 us
  Pallas kernels  102 us (97%)
  local copies, waits for them, and re-layouts  2.26 us (2%)
    pallas_call x1, Pallas kernels, body(): pl.pallas_call(kernel, out_shape=jax.ShapeDtypeStruct((B, C, K), bf16), i...  102 us
    unnamed x1, local copies, waits for them, and re-layouts  2.26 us

profile of v2, /device:TPU:8, one launch (start us, length us, event | category | flops | bytes accessed | tf_op | source)
XLA Modules:
  0.0 104.4 jit_solution(3879143578091635530)
XLA Ops:
  0.0 102.1 %shard_map.46 = bf16[64,64,64]{2,1,0:T(8,128)(2,1)} custom-call(bf16[64,64,64]{2,1,0:T(8,128)(2,1)} %coef.1, s32[8,1,64]{2,1,0:T(1,128)} %pairing_any.1, s32[8,1,64]{2,1,0:T(1,128)} %pairing_any.1, bf16[8,64,64,128]{3,2,1,0:T(8,128)(2,1)} %lw.1, bf16[64,64,64]{2,1,0:T(8,128)(2,1)} %mw.1), custom_call_target="tpu_custom_call" | custom-call | tf_op jit(solution)/shard_map/pallas_call | solution.py:336
  102.1 2.3 %copy.6 = bf16[64,64,64]{2,1,0:T(8,128)(2,1)} copy(bf16[64,64,64]{2,1,0:T(8,128)(2,1)} %shard_map.46) | data formatting | bytes 1048576

commit v3 on v2

v3 whole, which is shorter than its diff:
```python
import jax
import jax.numpy as jnp
from jax import lax
from jax.experimental import pallas as pl
from jax.experimental.pallas import tpu as pltpu
from jax.sharding import PartitionSpec as P

LEVELS = 8
N = 64
B = 64
K = 64
C = 64
Q = 4
H = C // Q
T = B // 2
PIECES = 2
PT = T // PIECES
X = 4
MESH = pl.DeviceIdType.MESH


def kernel(coef, pairing, pairing_any, lw, mw, out,
           x_in, w, m, w_x, m_x, m_send, pair_v, pair_s, y_out,
           in_sem, w_sem, m_sem, out_sem, pair_sem, own_sem,
           lvl_send, lvl_recv, a_send, a_recv, e_send, e_recv, wz_send, wz_recv, wx_send, wx_recv,
           *per_chunk):
    me = lax.axis_index("src")
    rhs = lax.axis_index("rhs")
    z = me // 8
    zb1 = (z // 2) % 2

    lists = [per_chunk[i * Q:(i + 1) * Q] for i in range(len(per_chunk) // Q)]
    s0, s1, s2, s3, s4, s5, s6, s7, r0, r1, r2, r3, r5, r6, r7, other5, moved, t4 = lists
    state, far_of = (s0, s1, s2, s3, s4, s5, s6, s7), (r0, r1, r2, r3, None, r5, r6, r7)

    load_x = pltpu.make_async_copy(coef, x_in, in_sem)
    load_x.start()
    load_w = [pltpu.make_async_copy(lw.at[l], w.at[l], w_sem.at[l]) for l in range(LEVELS)]
    load_m = pltpu.make_async_copy(mw, m, m_sem)
    load_m.start()

    def flipped(s, h):
        return s + (1 << h) * (1 - 2 * ((s // (1 << h)) % 2))

    e16, e32 = flipped(me, 4), flipped(me, 5)
    e48 = flipped(e16, 5)
    far_x = [(rhs + k) % X for k in range(1, X)]
    barrier = pltpu.get_barrier_semaphore()

    @pl.loop(1, N)
    def _(k):
        pl.semaphore_signal(barrier, inc=1, device_id=((me + k) % N, rhs), device_id_type=MESH)

    for x in far_x:
        pl.semaphore_signal(barrier, inc=1, device_id=(me, x), device_id_type=MESH)
    for l in range(LEVELS):
        load_w[l].start()

    def remote(src, dst, send, recv, dev, x=None):
        return pltpu.make_async_remote_copy(
            src_ref=src, dst_ref=dst, send_sem=send, recv_sem=recv,
            device_id=(dev, rhs if x is None else x), device_id_type=MESH)

    def level_copy(l, q, piece):
        tiles = pl.ds(piece * PT, PT)
        return remote(state[l][q].at[tiles], far_of[l][q].at[tiles],
                      lvl_send.at[l, q, piece], lvl_recv.at[l, q, piece], flipped(me, l % 6))

    def a2a_copy(q, i, e):
        return remote(s4[q].at[i], moved[q].at[me], a_send.at[q], a_recv.at[q], e)

    def a2a_own(q, i):
        return pltpu.make_async_copy(s4[q].at[i], moved[q].at[me], own_sem.at[q])

    def a2a_recv_all(q):
        return remote(moved[q].at[pl.ds(0, N - 1)], moved[q].at[pl.ds(0, N - 1)], a_send.at[q], a_recv.at[q], e16)

    def a2a_send_all(q, n):
        return remote(s4[q].at[pl.ds(0, n)], s4[q].at[pl.ds(0, n)], a_send.at[q], a_recv.at[q], e16)

    def far5_copy(q, piece):
        tiles = pl.ds(piece * PT, PT)
        return remote(s5[q].at[tiles], r5[q].at[tiles], e_send.at[0, q, piece], e_recv.at[0, q, piece], e32)

    def other_copies(q, piece):
        tiles = pl.ds(piece * PT, PT)
        src = other5[q].at[tiles]
        return (remote(src, r5[q].at[tiles], e_send.at[1, q, piece], e_recv.at[0, q, piece], e48),
                remote(src, s5[q].at[tiles], e_send.at[2, q, piece], e_recv.at[1, q, piece], e16))

    quarter_w, quarter_m = pl.ds(rhs * (B // X), B // X), pl.ds(rhs * (B // 2 // X), B // 2 // X)

    def weight_z():
        return [
            remote(m_send.at[quarter_m], m_x.at[quarter_m], wz_send.at[0], wz_recv.at[0], e16),
            remote(lw.at[4, quarter_w], w_x.at[quarter_w], wz_send.at[1], wz_recv.at[1], e16),
            remote(pairing_any, pair_v, wz_send.at[2], wz_recv.at[2], e16),
        ]

    def weight_x(which):
        ref, quarter = ((m_x, quarter_m), (w_x, quarter_w))[which]
        return [remote(ref.at[quarter], ref.at[quarter], wx_send.at[which, k], wx_recv.at[which, k], me, far_x[k])
                for k in range(X - 1)]

    low_w = lax.broadcasted_iota(jnp.int32, (K, 2 * K), 1) < K
    low_t = lax.broadcasted_iota(jnp.int32, (H, 2 * K), 1) < K

    def turned(x):
        return jnp.concatenate([x[:, K:], x[:, :K]], axis=1)

    def lo(x):
        return jnp.where(low_w, x, jnp.zeros_like(x))

    def hi(x):
        return jnp.where(low_w, jnp.zeros_like(x), x)

    def first_rows(pair):
        return jnp.concatenate([lo(pair), hi(pair)], axis=1)

    def second_rows(pair):
        back = turned(pair)
        return jnp.concatenate([hi(back), lo(back)], axis=1)

    def times(x, *rows):
        weight = jnp.concatenate(rows, axis=0)
        return lax.dot_general(x, weight, (((1,), (1,)), ((), ())), preferred_element_type=jnp.float32)

    def beside(own, far):
        return jnp.concatenate([own, far], axis=1)

    def bf16(x):
        return x.astype(jnp.bfloat16)

    def gathered(ref, p, half):
        tile = ref[(p // 32) * 16 + p % 16]
        return jnp.where((p // 16) % 2 == half, tile, turned(tile))

    def pair_level(l, q, i, b, swap=False):
        far = jnp.where(low_t, gathered(far_of[l][q], pairing[l, 0, b + 16], 0),
                        gathered(far_of[l][q], pairing[l, 0, b], 1))
        rows = first_rows(w[l, b]), second_rows(w[l, b + 16])
        return bf16(times(beside(state[l][q][i], far), *(rows[::-1] if swap else rows)))

    def begin(q):
        @pl.loop(0, PIECES)
        def _(piece):
            for j in range(PT):
                b = piece * 2 * PT + j
                s0[q][piece * PT + j] = beside(x_in[b, q * H:(q + 1) * H, :], x_in[b + 16, q * H:(q + 1) * H, :])
            level_copy(0, q, piece).start()

    def wait_level(l, q):
        @pl.loop(0, PIECES)
        def _(piece):
            level_copy(l, q, piece).wait_recv()

    def plain_level(l, q):
        @pl.loop(0, PIECES)
        def _(piece):
            for j in range(PT):
                i, b = piece * PT + j, piece * 2 * PT + j
                new = pair_level(l, q, i, b)
                if l < LEVELS - 1:
                    state[l + 1][q][i] = new
                else:
                    y_out[b, q * H:(q + 1) * H, :] = new[:, :K]
                    y_out[b + 16, q * H:(q + 1) * H, :] = new[:, K:]
            if l < LEVELS - 1:
                level_copy(l + 1, q, piece).start()

    def last_source_level(q):
        @pl.loop(0, PIECES)
        def _(step):
            piece = (step + z // 4) % PIECES
            for j in range(PT):
                i, b = piece * PT + j, piece * 2 * PT + j
                s4[q][i] = pair_level(3, q, i, b, swap=q % 2 == 1)

            @pl.loop(0, PT)
            def _(j):
                i = piece * PT + j
                e = piece * 2 * PT + j + 16 * (q % 2)

                @pl.when(e != me)
                def _():
                    a2a_copy(q, i, e).start()

                @pl.when(e == me)
                def _():
                    a2a_own(q, i).start()

    def middle_and_level4(q):
        a2a_recv_all(q).wait_recv()
        a2a_own(q, 0).wait()

        @pl.loop(0, 2)
        def _(part):
            for j in range(B // 4):
                d = part * (B // 4) + j
                theirs = m_x[d]
                zero = jnp.zeros((K, K), jnp.bfloat16)
                for s, other in ((d, hi(theirs)), (d + B // 2, hi(turned(theirs)))):
                    t4[q][s] = bf16(times(moved[q][s], beside(m[s], zero), other))

        @pl.loop(0, PIECES)
        def _(piece):
            for j in range(PT):
                i, first = piece * PT + j, piece * 2 * PT + j
                new = []
                for b, swap in ((first, False), (first + 16, True)):
                    far = jnp.where(low_t, t4[q][pair_s[4, 0, b]], t4[q][pairing[4, 0, b]])
                    rows = first_rows(w[4, b]), second_rows(w_x[b])
                    new.append(times(beside(t4[q][b], far), *(rows[::-1] if swap else rows)))
                s5[q][i] = bf16(jnp.where(low_t, new[0], new[1]))
                other5[q][i] = turned(bf16(jnp.where(low_t, new[1], new[0])))
            for copy in (far5_copy(q, piece),) + other_copies(q, piece):
                copy.start()

    def wait_level5(q):
        @pl.loop(0, PIECES)
        def _(piece):
            far5_copy(q, piece).wait_recv()

        @pl.when(zb1 != q % 2)
        def _():
            @pl.loop(0, PIECES)
            def _(piece):
                other_copies(q, piece)[1].wait_recv()

    waited = set()

    def need(*names):
        for name in names:
            if name not in waited:
                waited.add(name)
                if name == "m":
                    load_m.wait()
                elif name == "x":
                    for which in range(2):
                        for copy in weight_x(which):
                            copy.wait_recv()
                    to_smem = pltpu.make_async_copy(pair_v, pair_s, pair_sem)
                    to_smem.start()
                    to_smem.wait()
                else:
                    load_w[name].wait()

    def forward():
        for which, crossing in enumerate(weight_z()):
            crossing.wait_recv()
            if which < 2:
                for copy in weight_x(which):
                    copy.start()

    def store(q):
        rows = pl.ds(q * H, H)
        return pltpu.make_async_copy(y_out.at[:, rows], out.at[:, rows], out_sem.at[q])

    def task(t, q):
        if t == 4:
            need("m", "x", 4)

            @pl.when(zb1 == q % 2)
            def _():
                middle_and_level4(q)
        else:
            need(t)
            if t == 5:
                wait_level5(q)
            else:
                wait_level(t, q)
            if t == 3:
                last_source_level(q)
            else:
                plain_level(t, q)
            if t == 7:
                store(q).start()

    load_x.wait()
    pl.semaphore_wait(barrier, N - 1 + X - 1)
    for q in range(Q):
        begin(q)
    need("m")
    for d in range(B // 2):
        m_send[d] = beside(m[d + B // 2], m[d])
    for copy in weight_z():
        copy.start()
    for t in range(LEVELS):
        for q in range(Q):
            task(t, q)
            if (t, q) == (1, Q - 1):
                forward()

    for copy in weight_z() + weight_x(0) + weight_x(1):
        copy.wait_send()
    for q in range(Q):
        @pl.loop(0, PIECES)
        def _(piece):
            for l in (0, 1, 2, 3, 6, 7):
                level_copy(l, q, piece).wait_send()

        @pl.when(zb1 == q % 2)
        def _():
            @pl.loop(0, PIECES)
            def _(piece):
                for copy in (far5_copy(q, piece),) + other_copies(q, piece):
                    copy.wait_send()
            a2a_send_all(q, T - 1).wait_send()

        @pl.when(zb1 != q % 2)
        def _():
            a2a_send_all(q, T).wait_send()
    for q in range(Q):
        store(q).wait()


def body(coefficients, pairing, level_weights, middle_weights):
    bf16 = jnp.bfloat16
    dma = pltpu.SemaphoreType.DMA
    any_space = pl.BlockSpec(memory_space=pl.ANY)
    tiles = pltpu.VMEM((T, H, 2 * K), bf16)
    slots = pltpu.VMEM((B, H, 2 * K), bf16)
    return pl.pallas_call(
        kernel,
        out_shape=jax.ShapeDtypeStruct((B, C, K), bf16),
        in_specs=[any_space, pl.BlockSpec(memory_space=pltpu.SMEM), any_space, any_space, any_space],
        out_specs=any_space,
        scratch_shapes=[
            pltpu.VMEM((B, C, K), bf16),
            pltpu.VMEM((LEVELS, B, K, 2 * K), bf16),
            pltpu.VMEM((B, K, K), bf16),
            pltpu.VMEM((B, K, 2 * K), bf16),
            pltpu.VMEM((B // 2, K, 2 * K), bf16),
            pltpu.VMEM((B // 2, K, 2 * K), bf16),
            pltpu.VMEM((LEVELS, 1, B), jnp.int32),
            pltpu.SMEM((LEVELS, 1, B), jnp.int32),
            pltpu.VMEM((B, C, K), bf16),
            dma, dma((LEVELS,)), dma, dma((Q,)), dma, dma((Q,)),
            dma((LEVELS, Q, PIECES)), dma((LEVELS, Q, PIECES)), dma((Q,)), dma((Q,)),
            dma((3, Q, PIECES)), dma((2, Q, PIECES)), dma((3,)), dma((3,)), dma((2, X - 1)), dma((2, X - 1)),
        ] + [tiles] * (16 * Q) + [slots] * (2 * Q),
        compiler_params=pltpu.CompilerParams(
            collective_id=0, has_side_effects=True, vmem_limit_bytes=60 * 1024 * 1024),
    )(coefficients, pairing, pairing, level_weights, middle_weights)


def solution(mesh):
    placed = (
        P("src", "rhs", None),
        P(None, "src", None),
        P(None, "src", None, None),
        P("src", None, None),
    )
    return jax.shard_map(
        body, mesh=mesh, in_specs=placed, out_specs=P("src", "rhs", None), check_vma=False
    )
```

time: 105 us -> 102 us (0.971)
  the two profiles are of different devices: /device:TPU:8 before, /device:TPU:36 now
where the time goes in v3:
time: 102 us
  Pallas kernels  99.9 us (98%)
  local copies, waits for them, and re-layouts  2.26 us (2%)
    pallas_call x1, Pallas kernels, body(): pl.pallas_call(kernel, out_shape=jax.ShapeDtypeStruct((B, C, K), bf16), i...  99.9 us
    unnamed x1, local copies, waits for them, and re-layouts  2.26 us

profile of v3, /device:TPU:36, one launch (start us, length us, event | category | flops | bytes accessed | tf_op | source)
XLA Modules:
  0.0 102.2 jit_solution(14309391786538855303)
XLA Ops:
  0.0 99.9 %shard_map.46 = bf16[64,64,64]{2,1,0:T(8,128)(2,1)} custom-call(bf16[64,64,64]{2,1,0:T(8,128)(2,1)} %coef.1, s32[8,1,64]{2,1,0:T(1,128)} %pairing_any.1, s32[8,1,64]{2,1,0:T(1,128)} %pairing_any.1, bf16[8,64,64,128]{3,2,1,0:T(8,128)(2,1)} %lw.1, bf16[64,64,64]{2,1,0:T(8,128)(2,1)} %mw.1), custom_call_target="tpu_custom_call" | custom-call | tf_op jit(solution)/shard_map/pallas_call | solution.py:323
  99.9 2.3 %copy.6 = bf16[64,64,64]{2,1,0:T(8,128)(2,1)} copy(bf16[64,64,64]{2,1,0:T(8,128)(2,1)} %shard_map.46) | data formatting | bytes 1048576

commit v4 on v3

--- a/solution.py
+++ b/solution.py
@@ -17,12 +17,20 @@
 PT = T // PIECES
 X = 4
 MESH = pl.DeviceIdType.MESH
+M_PARTS, W_PARTS = 2, 4
+ORDER = (
+    (0, 0), (0, 1), (0, 2), (0, 3), (1, 0), (None, 0), (1, 1), (None, 1), (1, 2), (None, 2), (1, 3), (None, 3),
+    (2, 0), (None, 4), (2, 1), (None, 5), (2, 2), (2, 3), (3, 0), (3, 1), (3, 2), (3, 3), (4, 0), (4, 1), (4, 2), (4, 3),
+    (5, 0), (5, 1), (6, 0), (6, 1), (5, 2), (5, 3), (6, 2), (6, 3), (7, 0), (7, 1), (7, 2), (7, 3),
+)
+GATES = {}
+GATE5 = False
 
 
 def kernel(coef, pairing, pairing_any, lw, mw, out,
            x_in, w, m, w_x, m_x, m_send, pair_v, pair_s, y_out,
            in_sem, w_sem, m_sem, out_sem, pair_sem, own_sem,
-           lvl_send, lvl_recv, a_send, a_recv, e_send, e_recv, wz_send, wz_recv, wx_send, wx_recv,
+           lvl_send, lvl_recv, a_send, a_recv, e_send, e_recv, wz_send, wz_recv, wx_send, wx_recv, pz_sem,
            *per_chunk):
     me = lax.axis_index("src")
     rhs = lax.axis_index("rhs")
@@ -88,19 +96,24 @@
         return (remote(src, r5[q].at[tiles], e_send.at[1, q, piece], e_recv.at[0, q, piece], e48),
                 remote(src, s5[q].at[tiles], e_send.at[2, q, piece], e_recv.at[1, q, piece], e16))
 
-    quarter_w, quarter_m = pl.ds(rhs * (B // X), B // X), pl.ds(rhs * (B // 2 // X), B // 2 // X)
-
-    def weight_z():
-        return [
-            remote(m_send.at[quarter_m], m_x.at[quarter_m], wz_send.at[0], wz_recv.at[0], e16),
-            remote(lw.at[4, quarter_w], w_x.at[quarter_w], wz_send.at[1], wz_recv.at[1], e16),
-            remote(pairing_any, pair_v, wz_send.at[2], wz_recv.at[2], e16),
-        ]
-
-    def weight_x(which):
-        ref, quarter = ((m_x, quarter_m), (w_x, quarter_w))[which]
-        return [remote(ref.at[quarter], ref.at[quarter], wx_send.at[which, k], wx_recv.at[which, k], me, far_x[k])
+    def weight_part(part):
+        if part < M_PARTS:
+            blocks = T // X // M_PARTS
+            return m_send, m_x, pl.ds(rhs * (T // X) + part * blocks, blocks)
+        blocks = B // X // W_PARTS
+        return lw.at[4], w_x, pl.ds(rhs * (B // X) + (part - M_PARTS) * blocks, blocks)
+
+    def weight_z(part):
+        src, dst, blocks = weight_part(part)
+        return remote(src.at[blocks], dst.at[blocks], wz_send.at[part], wz_recv.at[part], e16)
+
+    def weight_x(part):
+        _, ref, blocks = weight_part(part)
+        return [remote(ref.at[blocks], ref.at[blocks], wx_send.at[part, k], wx_recv.at[part, k], me, far_x[k])
                 for k in range(X - 1)]
+
+    def pairing_z():
+        return remote(pairing_any, pair_v, pz_sem.at[0], pz_sem.at[1], e16)
 
     low_w = lax.broadcasted_iota(jnp.int32, (K, 2 * K), 1) < K
     low_t = lax.broadcasted_iota(jnp.int32, (H, 2 * K), 1) < K
@@ -154,7 +167,19 @@
         def _(piece):
             level_copy(l, q, piece).wait_recv()
 
+    left = set()
+
+    def wait_sent(l, q):
+        if (l, q) not in left:
+            left.add((l, q))
+
+            @pl.loop(0, PIECES)
+            def _(piece):
+                level_copy(l, q, piece).wait_send()
+
     def plain_level(l, q):
+        held = (l + 1, q) in GATES
+
         @pl.loop(0, PIECES)
         def _(piece):
             for j in range(PT):
@@ -165,7 +190,14 @@
                 else:
                     y_out[b, q * H:(q + 1) * H, :] = new[:, :K]
                     y_out[b + 16, q * H:(q + 1) * H, :] = new[:, K:]
-            if l < LEVELS - 1:
+            if l < LEVELS - 1 and not held:
+                level_copy(l + 1, q, piece).start()
+
+        if held:
+            wait_sent(*GATES[l + 1, q])
+
+            @pl.loop(0, PIECES)
+            def _(piece):
                 level_copy(l + 1, q, piece).start()
 
     def last_source_level(q):
@@ -189,7 +221,7 @@
                 def _():
                     a2a_own(q, i).start()
 
-    def middle_and_level4(q):
+    def middle(q):
         a2a_recv_all(q).wait_recv()
         a2a_own(q, 0).wait()
 
@@ -201,6 +233,22 @@
                 zero = jnp.zeros((K, K), jnp.bfloat16)
                 for s, other in ((d, hi(theirs)), (d + B // 2, hi(turned(theirs)))):
                     t4[q][s] = bf16(times(moved[q][s], beside(m[s], zero), other))
+
+    def send_level5(q, piece):
+        for copy in (far5_copy(q, piece),) + other_copies(q, piece):
+            copy.start()
+
+    def wait_sent5(q):
+        if (5, q) not in left:
+            left.add((5, q))
+
+            @pl.loop(0, PIECES)
+            def _(piece):
+                for copy in (far5_copy(q, piece),) + other_copies(q, piece):
+                    copy.wait_send()
+
+    def level4(q):
+        held = GATE5 and q >= 2
 
         @pl.loop(0, PIECES)
         def _(piece):
@@ -213,8 +261,15 @@
                     new.append(times(beside(t4[q][b], far), *(rows[::-1] if swap else rows)))
                 s5[q][i] = bf16(jnp.where(low_t, new[0], new[1]))
                 other5[q][i] = turned(bf16(jnp.where(low_t, new[1], new[0])))
-            for copy in (far5_copy(q, piece),) + other_copies(q, piece):
-                copy.start()
+            if not held:
+                send_level5(q, piece)
+
+        if held:
+            wait_sent5(q - 2)
+
+            @pl.loop(0, PIECES)
+            def _(piece):
+                send_level5(q, piece)
 
     def wait_level5(q):
         @pl.loop(0, PIECES)
@@ -233,24 +288,25 @@
         for name in names:
             if name not in waited:
                 waited.add(name)
-                if name == "m":
-                    load_m.wait()
-                elif name == "x":
-                    for which in range(2):
-                        for copy in weight_x(which):
+                if name == "m of e16":
+                    for part in range(M_PARTS):
+                        for copy in weight_x(part):
                             copy.wait_recv()
+                elif name == "w of e16":
+                    for part in range(M_PARTS, M_PARTS + W_PARTS):
+                        for copy in weight_x(part):
+                            copy.wait_recv()
+                    pairing_z().wait_recv()
                     to_smem = pltpu.make_async_copy(pair_v, pair_s, pair_sem)
                     to_smem.start()
                     to_smem.wait()
                 else:
                     load_w[name].wait()
 
-    def forward():
-        for which, crossing in enumerate(weight_z()):
-            crossing.wait_recv()
-            if which < 2:
-                for copy in weight_x(which):
-                    copy.start()
+    def forward(part):
+        weight_z(part).wait_recv()
+        for copy in weight_x(part):
+            copy.start()
 
     def store(q):
         rows = pl.ds(q * H, H)
@@ -258,11 +314,17 @@
 
     def task(t, q):
         if t == 4:
-            need("m", "x", 4)
+            need("m of e16")
 
             @pl.when(zb1 == q % 2)
             def _():
-                middle_and_level4(q)
+                middle(q)
+
+            need("w of e16", 4)
+
+            @pl.when(zb1 == q % 2)
+            def _():
+                level4(q)
         else:
             need(t)
             if t == 5:
@@ -276,35 +338,34 @@
             if t == 7:
                 store(q).start()
 
+    load_m.wait()
+    for d in range(T):
+        m_send[d] = beside(m[d + T], m[d])
     load_x.wait()
     pl.semaphore_wait(barrier, N - 1 + X - 1)
+    begin(0)
+    for part in range(M_PARTS + W_PARTS):
+        weight_z(part).start()
+    pairing_z().start()
+    for q in range(1, Q):
+        begin(q)
+    for t, q in ORDER:
+        if t is None:
+            forward(q)
+        else:
+            task(t, q)
+
+    pairing_z().wait_send()
+    for part in range(M_PARTS + W_PARTS):
+        for copy in [weight_z(part)] + weight_x(part):
+            copy.wait_send()
     for q in range(Q):
-        begin(q)
-    need("m")
-    for d in range(B // 2):
-        m_send[d] = beside(m[d + B // 2], m[d])
-    for copy in weight_z():
-        copy.start()
-    for t in range(LEVELS):
-        for q in range(Q):
-            task(t, q)
-            if (t, q) == (1, Q - 1):
-                forward()
-
-    for copy in weight_z() + weight_x(0) + weight_x(1):
-        copy.wait_send()
-    for q in range(Q):
-        @pl.loop(0, PIECES)
-        def _(piece):
-            for l in (0, 1, 2, 3, 6, 7):
-                level_copy(l, q, piece).wait_send()
+        for l in (0, 1, 2, 3, 6, 7):
+            wait_sent(l, q)
 
         @pl.when(zb1 == q % 2)
         def _():
-            @pl.loop(0, PIECES)
-            def _(piece):
-                for copy in (far5_copy(q, piece),) + other_copies(q, piece):
-                    copy.wait_send()
+            wait_sent5(q)
             a2a_send_all(q, T - 1).wait_send()
 
         @pl.when(zb1 != q % 2)
@@ -317,6 +378,7 @@
 def body(coefficients, pairing, level_weights, middle_weights):
     bf16 = jnp.bfloat16
     dma = pltpu.SemaphoreType.DMA
+    PARTS = M_PARTS + W_PARTS
     any_space = pl.BlockSpec(memory_space=pl.ANY)
     tiles = pltpu.VMEM((T, H, 2 * K), bf16)
     slots = pltpu.VMEM((B, H, 2 * K), bf16)
@@ -337,10 +399,10 @@
             pltpu.VMEM((B, C, K), bf16),
             dma, dma((LEVELS,)), dma, dma((Q,)), dma, dma((Q,)),
             dma((LEVELS, Q, PIECES)), dma((LEVELS, Q, PIECES)), dma((Q,)), dma((Q,)),
-            dma((3, Q, PIECES)), dma((2, Q, PIECES)), dma((3,)), dma((3,)), dma((2, X - 1)), dma((2, X - 1)),
+            dma((3, Q, PIECES)), dma((2, Q, PIECES)), dma((PARTS,)), dma((PARTS,)), dma((PARTS, X - 1)), dma((PARTS, X - 1)), dma((2,)),
         ] + [tiles] * (16 * Q) + [slots] * (2 * Q),
         compiler_params=pltpu.CompilerParams(
-            collective_id=0, has_side_effects=True, vmem_limit_bytes=60 * 1024 * 1024),
+            collective_id=0, has_side_effects=True, vmem_limit_bytes=52 * 1024 * 1024),
     )(coefficients, pairing, pairing, level_weights, middle_weights)
 
 

time: 102 us -> 96.8 us (0.949)
  the two profiles are of different devices: /device:TPU:36 before, /device:TPU:17 now
where the time goes in v4:
time: 96.8 us; the launch traced here: 96 us
  Pallas kernels  94.3 us (97%)
  local copies, waits for them, and re-layouts  1.66 us (2%)
    pallas_call x1, Pallas kernels, body(): pl.pallas_call(kernel, out_shape=jax.ShapeDtypeStruct((B, C, K), bf16), i...  94.3 us

profile of v4, /device:TPU:17, one launch (start us, length us, event | category | flops | bytes accessed | tf_op | source)
XLA Modules:
  0.0 96.0 jit_solution(10540994923122380140)
XLA Ops:
  0.0 0.0 copy-start
  0.0 0.7 copy-done
  0.7 94.3 %shard_map.46 = bf16[64,64,64]{2,1,0:T(8,128)(2,1)S(1)} custom-call(bf16[64,64,64]{2,1,0:T(8,128)(2,1)} %coef.1, s32[8,1,64]{2,1,0:T(1,128)S(1)} %copy-done, s32[8,1,64]{2,1,0:T(1,128)S(1)} %copy-done, bf16[8,64,64,128]{3,2,1,0:T(8,128)(2,1)} %lw.1, bf16[64,64,64]{2,1,0:T(8,128)(2,1)} %mw.1), custom_call_target="tpu_custom_call" | custom-call | tf_op jit(solution)/shard_map/pallas_call | solution.py:385
  95.0 1.0 %copy.6 = bf16[64,64,64]{2,1,0:T(8,128)(2,1)} copy(bf16[64,64,64]{2,1,0:T(8,128)(2,1)S(1)} %shard_map.46) | data formatting | bytes 1048576
Async XLA Ops:
  0.0 0.7 copy-start

commit v5 on v4

--- a/solution.py
+++ b/solution.py
@@ -19,12 +19,14 @@
 MESH = pl.DeviceIdType.MESH
 M_PARTS, W_PARTS = 2, 4
 ORDER = (
-    (0, 0), (0, 1), (0, 2), (0, 3), (1, 0), (None, 0), (1, 1), (None, 1), (1, 2), (None, 2), (1, 3), (None, 3),
-    (2, 0), (None, 4), (2, 1), (None, 5), (2, 2), (2, 3), (3, 0), (3, 1), (3, 2), (3, 3), (4, 0), (4, 1), (4, 2), (4, 3),
-    (5, 0), (5, 1), (6, 0), (6, 1), (5, 2), (5, 3), (6, 2), (6, 3), (7, 0), (7, 1), (7, 2), (7, 3),
+    (0, (0,)), (0, (1,)), (0, (2,)), (0, (3,)),
+    (1, (0,)), (None, 0), (1, (1,)), (None, 1), (1, (2,)), (None, 2), (1, (3,)), (None, 3),
+    (2, (0,)), (None, 4), (2, (1,)), (None, 5), (2, (2,)), (2, (3,)),
+    (3, (0,)), (3, (1,)), (3, (2,)), (3, (3,)),
+    (4, (0,)), (4, (1,)), (4, (2,)), (4, (3,)),
+    (5, (0,)), (6, (0,)), (5, (1,)), (6, (1,)), (5, (2,)), (6, (2,)), (5, (3,)), (6, (3,)),
+    (7, (0,)), (7, (1,)), (7, (2,)), (7, (3,)),
 )
-GATES = {}
-GATE5 = False
 
 
 def kernel(coef, pairing, pairing_any, lw, mw, out,
@@ -145,21 +147,28 @@
         return x.astype(jnp.bfloat16)
 
     def gathered(ref, p, half):
-        tile = ref[(p // 32) * 16 + p % 16]
-        return jnp.where((p // 16) % 2 == half, tile, turned(tile))
-
-    def pair_level(l, q, i, b, swap=False):
-        far = jnp.where(low_t, gathered(far_of[l][q], pairing[l, 0, b + 16], 0),
-                        gathered(far_of[l][q], pairing[l, 0, b], 1))
-        rows = first_rows(w[l, b]), second_rows(w[l, b + 16])
-        return bf16(times(beside(state[l][q][i], far), *(rows[::-1] if swap else rows)))
-
-    def begin(q):
+        tile = ref[((p >> 5) << 4) | (p & 15)]
+        return jnp.where(((p >> 4) & 1) == half, tile, turned(tile))
+
+    def pair_level(l, qs, i, b):
+        first, second = pairing[l, 0, b], pairing[l, 0, b + 16]
+        tiles = []
+        for q in qs:
+            far = jnp.where(low_t, gathered(far_of[l][q], second, 0), gathered(far_of[l][q], first, 1))
+            tiles.append(beside(state[l][q][i], far))
+        new = bf16(times(jnp.concatenate(tiles, axis=0), first_rows(w[l, b]), second_rows(w[l, b + 16])))
+        return [new[k * H:(k + 1) * H] for k in range(len(qs))]
+
+    def pack(q):
         @pl.loop(0, PIECES)
         def _(piece):
             for j in range(PT):
                 b = piece * 2 * PT + j
                 s0[q][piece * PT + j] = beside(x_in[b, q * H:(q + 1) * H, :], x_in[b + 16, q * H:(q + 1) * H, :])
+
+    def send_first(q):
+        @pl.loop(0, PIECES)
+        def _(piece):
             level_copy(0, q, piece).start()
 
     def wait_level(l, q):
@@ -167,59 +176,43 @@
         def _(piece):
             level_copy(l, q, piece).wait_recv()
 
-    left = set()
-
-    def wait_sent(l, q):
-        if (l, q) not in left:
-            left.add((l, q))
-
-            @pl.loop(0, PIECES)
-            def _(piece):
-                level_copy(l, q, piece).wait_send()
-
-    def plain_level(l, q):
-        held = (l + 1, q) in GATES
-
+    def plain_level(l, qs):
         @pl.loop(0, PIECES)
         def _(piece):
             for j in range(PT):
                 i, b = piece * PT + j, piece * 2 * PT + j
-                new = pair_level(l, q, i, b)
-                if l < LEVELS - 1:
-                    state[l + 1][q][i] = new
-                else:
-                    y_out[b, q * H:(q + 1) * H, :] = new[:, :K]
-                    y_out[b + 16, q * H:(q + 1) * H, :] = new[:, K:]
-            if l < LEVELS - 1 and not held:
-                level_copy(l + 1, q, piece).start()
-
-        if held:
-            wait_sent(*GATES[l + 1, q])
-
-            @pl.loop(0, PIECES)
-            def _(piece):
-                level_copy(l + 1, q, piece).start()
-
-    def last_source_level(q):
+                for q, new in zip(qs, pair_level(l, qs, i, b)):
+                    if l < LEVELS - 1:
+                        state[l + 1][q][i] = new
+                    else:
+                        y_out[b, q * H:(q + 1) * H, :] = new[:, :K]
+                        y_out[b + 16, q * H:(q + 1) * H, :] = new[:, K:]
+            if l < LEVELS - 1:
+                for q in qs:
+                    level_copy(l + 1, q, piece).start()
+
+    def last_source_level(qs):
         @pl.loop(0, PIECES)
         def _(step):
             piece = (step + z // 4) % PIECES
             for j in range(PT):
                 i, b = piece * PT + j, piece * 2 * PT + j
-                s4[q][i] = pair_level(3, q, i, b, swap=q % 2 == 1)
+                for q, new in zip(qs, pair_level(3, qs, i, b)):
+                    s4[q][i] = turned(new) if q % 2 else new
 
             @pl.loop(0, PT)
             def _(j):
                 i = piece * PT + j
-                e = piece * 2 * PT + j + 16 * (q % 2)
-
-                @pl.when(e != me)
-                def _():
-                    a2a_copy(q, i, e).start()
-
-                @pl.when(e == me)
-                def _():
-                    a2a_own(q, i).start()
+                for q in qs:
+                    e = piece * 2 * PT + j + 16 * (q % 2)
+
+                    @pl.when(e != me)
+                    def _():
+                        a2a_copy(q, i, e).start()
+
+                    @pl.when(e == me)
+                    def _():
+                        a2a_own(q, i).start()
 
     def middle(q):
         a2a_recv_all(q).wait_recv()
@@ -234,22 +227,7 @@
                 for s, other in ((d, hi(theirs)), (d + B // 2, hi(turned(theirs)))):
                     t4[q][s] = bf16(times(moved[q][s], beside(m[s], zero), other))
 
-    def send_level5(q, piece):
-        for copy in (far5_copy(q, piece),) + other_copies(q, piece):
-            copy.start()
-
-    def wait_sent5(q):
-        if (5, q) not in left:
-            left.add((5, q))
-
-            @pl.loop(0, PIECES)
-            def _(piece):
-                for copy in (far5_copy(q, piece),) + other_copies(q, piece):
-                    copy.wait_send()
-
     def level4(q):
-        held = GATE5 and q >= 2
-
         @pl.loop(0, PIECES)
         def _(piece):
             for j in range(PT):
@@ -261,15 +239,8 @@
                     new.append(times(beside(t4[q][b], far), *(rows[::-1] if swap else rows)))
                 s5[q][i] = bf16(jnp.where(low_t, new[0], new[1]))
                 other5[q][i] = turned(bf16(jnp.where(low_t, new[1], new[0])))
-            if not held:
-                send_level5(q, piece)
-
-        if held:
-            wait_sent5(q - 2)
-
-            @pl.loop(0, PIECES)
-            def _(piece):
-                send_level5(q, piece)
+            for copy in (far5_copy(q, piece),) + other_copies(q, piece):
+                copy.start()
 
     def wait_level5(q):
         @pl.loop(0, PIECES)
@@ -312,60 +283,73 @@
         rows = pl.ds(q * H, H)
         return pltpu.make_async_copy(y_out.at[:, rows], out.at[:, rows], out_sem.at[q])
 
-    def task(t, q):
+    def task(t, qs):
         if t == 4:
             need("m of e16")
-
-            @pl.when(zb1 == q % 2)
-            def _():
-                middle(q)
+            for q in qs:
+                @pl.when(zb1 == q % 2)
+                def _():
+                    middle(q)
 
             need("w of e16", 4)
-
-            @pl.when(zb1 == q % 2)
-            def _():
-                level4(q)
-        else:
-            need(t)
+            for q in qs:
+                @pl.when(zb1 == q % 2)
+                def _():
+                    level4(q)
+            return
+        need(t)
+        for q in qs:
             if t == 5:
                 wait_level5(q)
             else:
                 wait_level(t, q)
-            if t == 3:
-                last_source_level(q)
-            else:
-                plain_level(t, q)
-            if t == 7:
+        if t == 3:
+            last_source_level(qs)
+        else:
+            plain_level(t, qs)
+        if t == 7:
+            for q in qs:
                 store(q).start()
 
+    load_x.wait()
+    pack(0)
+    pl.semaphore_wait(barrier, N - 1 + X - 1)
+    send_first(0)
+    for part in range(M_PARTS, M_PARTS + W_PARTS):
+        weight_z(part).start()
+    pairing_z().start()
+    pack(1)
+    send_first(1)
     load_m.wait()
     for d in range(T):
         m_send[d] = beside(m[d + T], m[d])
-    load_x.wait()
-    pl.semaphore_wait(barrier, N - 1 + X - 1)
-    begin(0)
-    for part in range(M_PARTS + W_PARTS):
+    for part in range(M_PARTS):
         weight_z(part).start()
-    pairing_z().start()
-    for q in range(1, Q):
-        begin(q)
-    for t, q in ORDER:
+    for q in range(2, Q):
+        pack(q)
+        send_first(q)
+    for t, what in ORDER:
         if t is None:
-            forward(q)
+            forward(what)
         else:
-            task(t, q)
+            task(t, what)
 
     pairing_z().wait_send()
     for part in range(M_PARTS + W_PARTS):
         for copy in [weight_z(part)] + weight_x(part):
             copy.wait_send()
     for q in range(Q):
-        for l in (0, 1, 2, 3, 6, 7):
-            wait_sent(l, q)
+        @pl.loop(0, PIECES)
+        def _(piece):
+            for l in (0, 1, 2, 3, 6, 7):
+                level_copy(l, q, piece).wait_send()
 
         @pl.when(zb1 == q % 2)
         def _():
-            wait_sent5(q)
+            @pl.loop(0, PIECES)
+            def _(piece):
+                for copy in (far5_copy(q, piece),) + other_copies(q, piece):
+                    copy.wait_send()
             a2a_send_all(q, T - 1).wait_send()
 
         @pl.when(zb1 != q % 2)

time: 96.8 us -> 101 us (1.043)
  the two profiles are of different devices: /device:TPU:17 before, /device:TPU:70 now
where the time goes in v5:
time: 101 us
  Pallas kernels  99 us (98%)
  local copies, waits for them, and re-layouts  1.66 us (2%)
    pallas_call x1, Pallas kernels, body(): pl.pallas_call(kernel, out_shape=jax.ShapeDtypeStruct((B, C, K), bf16), i...  99 us

profile of v5, /device:TPU:70, one launch (start us, length us, event | category | flops | bytes accessed | tf_op | source)
XLA Modules:
  0.0 100.6 jit_solution(12790669589686767865)
XLA Ops:
  0.0 0.0 copy-start
  0.0 0.7 copy-done
  0.7 99.0 %shard_map.46 = bf16[64,64,64]{2,1,0:T(8,128)(2,1)S(1)} custom-call(bf16[64,64,64]{2,1,0:T(8,128)(2,1)} %coef.1, s32[8,1,64]{2,1,0:T(1,128)S(1)} %copy-done, s32[8,1,64]{2,1,0:T(1,128)S(1)} %copy-done, bf16[8,64,64,128]{3,2,1,0:T(8,128)(2,1)} %lw.1, bf16[64,64,64]{2,1,0:T(8,128)(2,1)} %mw.1), custom_call_target="tpu_custom_call" | custom-call | tf_op jit(solution)/shard_map/pallas_call | solution.py:369
  99.7 1.0 copy.6
Async XLA Ops:
  0.0 0.7 copy-start

commit v6 on v5

--- a/solution.py
+++ b/solution.py
@@ -18,10 +18,11 @@
 X = 4
 MESH = pl.DeviceIdType.MESH
 M_PARTS, W_PARTS = 2, 4
+FIRST = 2
 ORDER = (
-    (0, (0,)), (0, (1,)), (0, (2,)), (0, (3,)),
-    (1, (0,)), (None, 0), (1, (1,)), (None, 1), (1, (2,)), (None, 2), (1, (3,)), (None, 3),
-    (2, (0,)), (None, 4), (2, (1,)), (None, 5), (2, (2,)), (2, (3,)),
+    (0, (0,)), (0, (1,)), ("z", 2), ("z", 3), (0, (2,)), (0, (3,)), ("z", 4), ("z", 5),
+    (1, (0,)), ("x", 0), (1, (1,)), ("x", 1), (1, (2,)), (1, (3,)), ("x", 2), ("x", 3),
+    (2, (0,)), ("x", 4), (2, (1,)), ("x", 5), (2, (2,)), (2, (3,)),
     (3, (0,)), (3, (1,)), (3, (2,)), (3, (3,)),
     (4, (0,)), (4, (1,)), (4, (2,)), (4, (3,)),
     (5, (0,)), (6, (0,)), (5, (1,)), (6, (1,)), (5, (2,)), (6, (2,)), (5, (3,)), (6, (3,)),
@@ -311,25 +312,23 @@
             for q in qs:
                 store(q).start()
 
+    load_m.wait()
+    for d in range(T):
+        m_send[d] = beside(m[d + T], m[d])
     load_x.wait()
     pack(0)
     pl.semaphore_wait(barrier, N - 1 + X - 1)
     send_first(0)
-    for part in range(M_PARTS, M_PARTS + W_PARTS):
+    for part in range(FIRST):
         weight_z(part).start()
     pairing_z().start()
-    pack(1)
-    send_first(1)
-    load_m.wait()
-    for d in range(T):
-        m_send[d] = beside(m[d + T], m[d])
-    for part in range(M_PARTS):
-        weight_z(part).start()
-    for q in range(2, Q):
+    for q in range(1, Q):
         pack(q)
         send_first(q)
     for t, what in ORDER:
-        if t is None:
+        if t == "z":
+            weight_z(what).start()
+        elif t == "x":
             forward(what)
         else:
             task(t, what)

time: 101 us -> 94.2 us (0.933)
  the two profiles are of different devices: /device:TPU:70 before, /device:TPU:17 now
where the time goes in v6:
time: 94.2 us; the launch traced here: 94.1 us
  Pallas kernels  92.5 us (98%)
  local copies, waits for them, and re-layouts  1.66 us (2%)
    pallas_call x1, Pallas kernels, body(): pl.pallas_call(kernel, out_shape=jax.ShapeDtypeStruct((B, C, K), bf16), i...  92.5 us

profile of v6, /device:TPU:17, one launch (start us, length us, event | category | flops | bytes accessed | tf_op | source)
XLA Modules:
  0.0 94.1 jit_solution(8951957962415801778)
XLA Ops:
  0.0 0.0 copy-start
  0.0 0.7 copy-done
  0.7 92.5 %shard_map.46 = bf16[64,64,64]{2,1,0:T(8,128)(2,1)S(1)} custom-call(bf16[64,64,64]{2,1,0:T(8,128)(2,1)} %coef.1, s32[8,1,64]{2,1,0:T(1,128)S(1)} %copy-done, s32[8,1,64]{2,1,0:T(1,128)S(1)} %copy-done, bf16[8,64,64,128]{3,2,1,0:T(8,128)(2,1)} %lw.1, bf16[64,64,64]{2,1,0:T(8,128)(2,1)} %mw.1), custom_call_target="tpu_custom_call" | custom-call | tf_op jit(solution)/shard_map/pallas_call | solution.py:368
  93.1 1.0 %copy.6 = bf16[64,64,64]{2,1,0:T(8,128)(2,1)} copy(bf16[64,64,64]{2,1,0:T(8,128)(2,1)S(1)} %shard_map.46) | data formatting | bytes 1048576
Async XLA Ops:
  0.0 0.7 copy-start

commit v7 on v6

--- a/solution.py
+++ b/solution.py
@@ -17,12 +17,12 @@
 PT = T // PIECES
 X = 4
 MESH = pl.DeviceIdType.MESH
-M_PARTS, W_PARTS = 2, 4
-FIRST = 2
+M_PARTS, W_PARTS = 1, 2
+FIRST = 1
 ORDER = (
-    (0, (0,)), (0, (1,)), ("z", 2), ("z", 3), (0, (2,)), (0, (3,)), ("z", 4), ("z", 5),
-    (1, (0,)), ("x", 0), (1, (1,)), ("x", 1), (1, (2,)), (1, (3,)), ("x", 2), ("x", 3),
-    (2, (0,)), ("x", 4), (2, (1,)), ("x", 5), (2, (2,)), (2, (3,)),
+    (0, (0,)), (0, (1,)), ("z", 1), (0, (2,)), (0, (3,)), ("z", 2),
+    (1, (0,)), (1, (1,)), ("x", 0), (1, (2,)), (1, (3,)), ("x", 1),
+    (2, (0,)), (2, (1,)), ("x", 2), (2, (2,)), (2, (3,)),
     (3, (0,)), (3, (1,)), (3, (2,)), (3, (3,)),
     (4, (0,)), (4, (1,)), (4, (2,)), (4, (3,)),
     (5, (0,)), (6, (0,)), (5, (1,)), (6, (1,)), (5, (2,)), (6, (2,)), (5, (3,)), (6, (3,)),
@@ -176,6 +176,10 @@
         @pl.loop(0, PIECES)
         def _(piece):
             level_copy(l, q, piece).wait_recv()
+
+    def store(q, piece):
+        blocks, rows = pl.ds(piece * 2 * PT, 2 * PT), pl.ds(q * H, H)
+        return pltpu.make_async_copy(y_out.at[blocks, rows], out.at[blocks, rows], out_sem.at[q, piece])
 
     def plain_level(l, qs):
         @pl.loop(0, PIECES)
@@ -191,6 +195,9 @@
             if l < LEVELS - 1:
                 for q in qs:
                     level_copy(l + 1, q, piece).start()
+            else:
+                for q in qs:
+                    store(q, piece).start()
 
     def last_source_level(qs):
         @pl.loop(0, PIECES)
@@ -280,10 +287,6 @@
         for copy in weight_x(part):
             copy.start()
 
-    def store(q):
-        rows = pl.ds(q * H, H)
-        return pltpu.make_async_copy(y_out.at[:, rows], out.at[:, rows], out_sem.at[q])
-
     def task(t, qs):
         if t == 4:
             need("m of e16")
@@ -308,10 +311,6 @@
             last_source_level(qs)
         else:
             plain_level(t, qs)
-        if t == 7:
-            for q in qs:
-                store(q).start()
-
     load_m.wait()
     for d in range(T):
         m_send[d] = beside(m[d + T], m[d])
@@ -355,7 +354,9 @@
         def _():
             a2a_send_all(q, T).wait_send()
     for q in range(Q):
-        store(q).wait()
+        @pl.loop(0, PIECES)
+        def _(piece):
+            store(q, piece).wait()
 
 
 def body(coefficients, pairing, level_weights, middle_weights):
@@ -380,7 +381,7 @@
             pltpu.VMEM((LEVELS, 1, B), jnp.int32),
             pltpu.SMEM((LEVELS, 1, B), jnp.int32),
             pltpu.VMEM((B, C, K), bf16),
-            dma, dma((LEVELS,)), dma, dma((Q,)), dma, dma((Q,)),
+            dma, dma((LEVELS,)), dma, dma((Q, PIECES)), dma, dma((Q,)),
             dma((LEVELS, Q, PIECES)), dma((LEVELS, Q, PIECES)), dma((Q,)), dma((Q,)),
             dma((3, Q, PIECES)), dma((2, Q, PIECES)), dma((PARTS,)), dma((PARTS,)), dma((PARTS, X - 1)), dma((PARTS, X - 1)), dma((2,)),
         ] + [tiles] * (16 * Q) + [slots] * (2 * Q),

time: 94.2 us -> 94.2 us (level)
  no operation moved by 1% of the time
where the time goes in v7:
time: 94.2 us; the launch traced here: 94.1 us
  Pallas kernels  92.4 us (98%)
  local copies, waits for them, and re-layouts  1.66 us (2%)
    pallas_call x1, Pallas kernels, body(): pl.pallas_call(kernel, out_shape=jax.ShapeDtypeStruct((B, C, K), bf16), i...  92.4 us

profile of v7, /device:TPU:17, one launch (start us, length us, event | category | flops | bytes accessed | tf_op | source)
XLA Modules:
  0.0 94.1 jit_solution(9673561679649850132)
XLA Ops:
  0.0 0.0 copy-start
  0.0 0.7 copy-done
  0.7 92.4 %shard_map.46 = bf16[64,64,64]{2,1,0:T(8,128)(2,1)S(1)} custom-call(bf16[64,64,64]{2,1,0:T(8,128)(2,1)} %coef.1, s32[8,1,64]{2,1,0:T(1,128)S(1)} %copy-done, s32[8,1,64]{2,1,0:T(1,128)S(1)} %copy-done, bf16[8,64,64,128]{3,2,1,0:T(8,128)(2,1)} %lw.1, bf16[64,64,64]{2,1,0:T(8,128)(2,1)} %mw.1), custom_call_target="tpu_custom_call" | custom-call | tf_op jit(solution)/shard_map/pallas_call | solution.py:369
  93.1 1.0 %copy.6 = bf16[64,64,64]{2,1,0:T(8,128)(2,1)} copy(bf16[64,64,64]{2,1,0:T(8,128)(2,1)S(1)} %shard_map.46) | data formatting | bytes 1048576
Async XLA Ops:
  0.0 0.7 copy-start
